TPU v7x, 512 devices: a whole 4x8x8 slice. The times are simulated.
512 devices in a mesh: seq: 64 (over x, z_hi, y), ch: 8 (over z_lo, core).
Axes of the slice: x: 4, y: 8, z: 8 (z_hi: 2, z_lo: 4; z = z_hi * 4 + z_lo), core: 2. Of those that a mesh axis runs over, the one named last changes fastest.
Arguments:
- gate_input: bfloat16 [16384, 4096], P('seq', 'ch'), may hold values from -6 to 6
- key_input: bfloat16 [16384, 4096], P('seq', 'ch'), may hold values from -6 to 6
- value_input: bfloat16 [16384, 4096], P('seq', 'ch'), may hold values from -6 to 6
- decay_rate: float32 [4096, 16], P('ch'), as said below
- residues: float32 [4096, 16], P('ch'), may hold values from -1.5 to 1.5
- out_weight: bfloat16 [4096, 4096], P('ch', 'seq'), may hold values from -0.09375 to 0.09375
Outputs:
- mixed: bfloat16 [16384, 4096], P(('seq', 'ch'))
Inputs may be any that keep to these rules, and one draw needn't show every extreme that they name: `decay_rate`: every entry is positive and at most 0.05.
All inputs are finite; a program needn't handle non-finite values.
Results may differ from a plain program's by a relative error of at most 0.025.
Values may be sent and summed in bfloat16 or wider, within the bound.
No kernel may reach another device: no remote copies, remote signals or barrier semaphores. Data moves between devices by JAX's collectives and lax.ppermute only.
A program may use at most 64 MiB of HBM per device.

v0:
```python
import jax
import jax.numpy as jnp
from jax import lax
from jax.experimental import pallas as pl
from jax.experimental.pallas import tpu as pltpu
from jax.sharding import Mesh, PartitionSpec as P

AXES = (("x", 4), ("h", 2), ("y", 8), ("z", 4), ("c", 2))
NX, NH, NY, NZ, NC = (size for _, size in AXES)
SEQ = ("x", "h", "y")
CH = ("z", "c")

SUB = 8
LANES = 128
f32 = jnp.float32
bf16 = jnp.bfloat16


def fill_signal(key_ref, value_ref, signal):
    for tile in range(signal.shape[0]):
        lanes = pl.ds(tile * LANES, LANES)
        signal[tile] = key_ref[:, lanes].astype(f32) * value_ref[:, lanes].astype(f32)


def run_states_kernel(key_ref, value_ref, rate_ref, runs_ref, block_ref, signal):
    poles, chans = rate_ref.shape
    steps = key_ref.shape[0] // SUB
    fill_signal(key_ref, value_ref, signal)
    later = (SUB - 1 - lax.broadcasted_iota(jnp.int32, (SUB, LANES), 0)).astype(f32) * steps
    for tile in range(chans // LANES):
        lanes = pl.ds(tile * LANES, LANES)
        rates = [jnp.broadcast_to(rate_ref[pl.ds(r, 1), lanes], (SUB, LANES)) for r in range(poles)]
        decays = [jnp.exp(-rate) for rate in rates]

        def step(j, states):
            x = signal[tile, pl.ds(j, SUB, stride=steps), :]
            return tuple(d * s + x for d, s in zip(decays, states))

        states = lax.fori_loop(0, steps, step, (jnp.zeros((SUB, LANES), f32),) * poles, unroll=4)
        for r in range(poles):
            runs_ref[r, :, lanes] = states[r]
            block_ref[pl.ds(r, 1), lanes] = jnp.sum(
                states[r] * jnp.exp(-rates[r] * later), axis=0, keepdims=True
            )


def run_states(key_input, value_input, rate):
    poles, chans = rate.shape
    return pl.pallas_call(
        run_states_kernel,
        out_shape=(
            jax.ShapeDtypeStruct((poles, SUB, chans), f32),
            jax.ShapeDtypeStruct((poles, chans), f32),
        ),
        scratch_shapes=[pltpu.VMEM((chans // LANES, key_input.shape[0], LANES), f32)],
        compiler_params=pltpu.CompilerParams(vmem_limit_bytes=32 << 20),
        name="run_states",
    )(key_input, value_input, rate)


def gated_kernel(gate_ref, key_ref, value_ref, rate_ref, residue_ref, runs_ref, before_ref, out_ref, signal, conv):
    poles, chans = rate_ref.shape
    steps = key_ref.shape[0] // SUB
    fill_signal(key_ref, value_ref, signal)
    run = lax.broadcasted_iota(jnp.int32, (SUB, LANES), 0)
    run_f = run.astype(f32)
    for tile in range(chans // LANES):
        lanes = pl.ds(tile * LANES, LANES)
        decays, weights, starts = [], [], []
        for r in range(poles):
            rate = jnp.broadcast_to(rate_ref[pl.ds(r, 1), lanes], (SUB, LANES))
            residue = jnp.broadcast_to(residue_ref[pl.ds(r, 1), lanes], (SUB, LANES))
            before = jnp.broadcast_to(before_ref[pl.ds(r, 1), lanes], (SUB, LANES))
            ends = runs_ref[r, :, lanes]
            for back in (1, 2, 4):
                moved = jnp.where(run >= back, pltpu.roll(ends, back, 0), 0.0)
                ends = ends + jnp.exp(-rate * (steps * back)) * moved
            start = jnp.where(run >= 1, pltpu.roll(ends, 1, 0), 0.0)
            starts.append(start + jnp.exp(-rate * (steps * run_f)) * before)
            decays.append(jnp.exp(-rate))
            weights.append(residue * jnp.sqrt(rate))

        def step(j, states):
            at = pl.ds(j, SUB, stride=steps)
            x = signal[tile, at, :]
            states = tuple(d * s + x for d, s in zip(decays, states))
            terms = [w * s for w, s in zip(weights, states)]
            while len(terms) > 1:
                terms = [a + b for a, b in zip(terms[::2], terms[1::2])]
            conv[tile, at, :] = terms[0]
            return states

        lax.fori_loop(0, steps, step, tuple(starts), unroll=4)
    rows = 32
    for part in range(gate_ref.shape[0] // rows):
        at = pl.ds(part * rows, rows)
        for tile in range(chans // LANES):
            lanes = pl.ds(tile * LANES, LANES)
            piece = (gate_ref[at, lanes].astype(f32) * conv[tile, at, :]).astype(bf16)
            for copy in range(NX):
                out_ref[copy, part % NC, pl.ds(part // NC * rows, rows), lanes] = piece


def gated_rows(gate_input, key_input, value_input, rate, residue, runs, before):
    length, chans = gate_input.shape
    return pl.pallas_call(
        gated_kernel,
        out_shape=jax.ShapeDtypeStruct((NX, NC, length // NC, chans), bf16),
        scratch_shapes=[pltpu.VMEM((chans // LANES, length, LANES), f32)] * 2,
        compiler_params=pltpu.CompilerParams(vmem_limit_bytes=32 << 20),
        name="gated_rows",
    )(gate_input, key_input, value_input, rate, residue, runs, before)


def swap(array, axis):
    return lax.ppermute(array, axis, [(0, 1), (1, 0)])


def exchange(array, axes):
    return lax.all_to_all(array, axes, 0, 0, tiled=True)


def copies(array, count):
    return jnp.broadcast_to(array[None], (count, *array.shape))


def state_before(block, rate, length):
    x, h, y = (lax.axis_index(axis) for axis in SEQ)
    blocks = exchange(copies(block, NY), "y")
    at = jnp.arange(NY)[:, None, None]
    back = y - 1 - at
    inner = jnp.sum(
        jnp.where(back >= 0, jnp.exp(-rate * (length * jnp.maximum(back, 0)).astype(f32)), 0.0) * blocks, axis=0
    )
    total = jnp.sum(jnp.exp(-rate * (length * (NY - 1 - at)).astype(f32)) * blocks, axis=0)
    totals = exchange(copies(total, NX * NH), ("x", "h"))
    back = x * NH + h - 1 - jnp.arange(NX * NH)[:, None, None]
    outer = jnp.sum(
        jnp.where(back >= 0, jnp.exp(-rate * (length * NY * jnp.maximum(back, 0)).astype(f32)), 0.0) * totals, axis=0
    )
    return inner + jnp.exp(-rate * (length * y).astype(f32)) * outer


def weight_columns(out_weight):
    h = lax.axis_index("h")
    mine = out_weight.T
    other = swap(mine, "h")
    pair = jnp.where(h == 0, jnp.stack([mine, other]), jnp.stack([other, mine]))
    gathered = lax.all_gather(pair, "y", axis=0, tiled=False)
    own = gathered.transpose(1, 0, 2, 3).reshape(-1, mine.shape[1])
    return own, swap(own, "c")


def body(gate_input, key_input, value_input, decay_rate, residues, out_weight):
    length, chans = gate_input.shape
    rate, residue = decay_rate.T, residues.T
    own_weight, other_weight = weight_columns(out_weight)
    runs, block = run_states(key_input, value_input, rate)
    before = state_before(block, rate, length)
    rows = gated_rows(gate_input, key_input, value_input, rate, residue, runs, before)
    arrived = exchange(rows.reshape(NX * NC, length // NC, chans), ("x", "c"))
    arrived = arrived.reshape(NX, NC, length // NC, chans)
    core = lax.axis_index("c")
    own = lax.dynamic_index_in_dim(arrived, core, 1, keepdims=False).reshape(-1, chans)
    other = lax.dynamic_index_in_dim(arrived, 1 - core, 1, keepdims=False).reshape(-1, chans)
    contract = (((1,), (1,)), ((), ()))
    partial = lax.dot_general(own, own_weight, contract, preferred_element_type=f32) + lax.dot_general(
        other, other_weight, contract, preferred_element_type=f32
    )
    columns = partial.shape[1]
    parts = exchange(partial.astype(bf16).reshape(NX * NZ, -1, columns), ("x", "z"))
    mixed = parts.reshape(NX, NZ, -1, columns).astype(f32).sum(axis=1).astype(bf16)
    return mixed.transpose(1, 0, 2).reshape(-1, NX * columns)


def solution(mesh):
    names, sizes = zip(*AXES)
    fine = Mesh(mesh.devices.reshape(sizes), names)
    return jax.shard_map(
        body,
        mesh=fine,
        in_specs=(P(SEQ, CH), P(SEQ, CH), P(SEQ, CH), P(CH, None), P(CH, None), P(CH, SEQ)),
        out_specs=P(SEQ + CH, None),
        check_vma=False,
    )
```

profile of v0, /device:TPU:1, one launch (start us, length us, event | category | flops | bytes accessed | tf_op | source)
XLA Modules:
  0.0 132.7 jit_solution(17180247165155722228)
XLA Ops:
  6.5 0.0 copy-start.5
  6.5 0.0 copy-start.1
  6.5 0.0 copy-start.7
  6.5 0.0 all-gather.2.cloned.1.call-start
  6.5 11.6 %collective-permute-start = (bf16[64,512]{1,0:T(8,128)(2,1)}, bf16[64,512]{1,0:T(8,128)(2,1)S(1)}, u32[]{:S(2)}, u32[]{:S(2)}) collective-permute-start(bf16[64,512]{1,0:T(8,128)(2,1)} %bitcast.36), channel_id=1, source_target_pairs={{0,64},{64,0},{1,65},{65,1},{2,66},{66,2},{3,67},{67,3},{4,68},{68... | collective-permute-start | bytes 196616 | tf_op jit(solution)/shard_map/ppermute | solution.py:116
  18.2 1.9 %collective-permute-done = bf16[64,512]{1,0:T(8,128)(2,1)S(1)} collective-permute-done((bf16[64,512]{1,0:T(8,128)(2,1)}, bf16[64,512]{1,0:T(8,128)(2,1)S(1)}, u32[]{:S(2)}, u32[]{:S(2)}) %collective-permute-start) | collective-permute-done | bytes 65568 | tf_op jit(solution)/shard_map/ppermute | solution.py:116
  20.1 1.6 %maximum_select_fusion = bf16[1,2,64,512]{3,2,0,1:T(8,128)(2,1)} fusion(bf16[1,1,64,512]{3,2,0,1:T(8,128)(2,1)S(1)} %bitcast.38, bf16[1,1,64,512]{3,2,0,1:T(8,128)(2,1)} %bitcast.37, pred[]{:T(512)S(6)} %eq.3), kind=kLoop, calls=%fused_computation.5 | loop fusion | flops 196608 | bytes 262145 | tf_op jit(solution)/shard_map/jit(_where)/select_n | solution.py:148
  21.6 0.0 all-gather.2.cloned.1.call-update
  21.7 0.0 copy-start
  21.7 0.9 copy-done
  22.6 0.0 copy-start.2
  22.6 0.9 copy-done.2
  23.6 0.0 copy-start.4
  23.6 0.8 copy-done.4
  24.3 0.0 copy-start.3
  24.3 0.0 copy-start.6
  24.3 1.2 run_states.1
  25.5 0.7 broadcast_in_dim.37
  26.2 6.8 %all-to-all-start = ((f32[8,16,512]{2,1,0:T(8,128)}), f32[8,16,512]{2,1,0:T(8,128)S(1)}, u32[]{:S(2)}, u32[]{:S(2)}) async-start(f32[8,16,512]{2,1,0:T(8,128)} %broadcast_in_dim.37), calls=%async_computation | async-start | bytes 524288 | tf_op jit(solution)/shard_map/all_to_all | solution.py:120
  33.1 0.8 bitcast_negate_fusion
  33.8 8.6 %all-to-all-done = f32[8,16,512]{2,1,0:T(8,128)S(1)} async-done(((f32[8,16,512]{2,1,0:T(8,128)}), f32[8,16,512]{2,1,0:T(8,128)S(1)}, u32[]{:S(2)}, u32[]{:S(2)}) %all-to-all-start) | async-done | bytes 262176 | tf_op jit(solution)/shard_map/all_to_all | solution.py:120
  42.4 0.2 multiply_reduce_fusion.1
  42.6 0.7 broadcast_in_dim.39
  43.4 9.2 %all-to-all-start.1 = ((f32[8,16,512]{2,1,0:T(8,128)}), f32[8,16,512]{2,1,0:T(8,128)S(1)}, u32[]{:S(2)}, u32[]{:S(2)}) async-start(f32[8,16,512]{2,1,0:T(8,128)} %broadcast_in_dim.39), calls=%async_computation.1 | async-start | bytes 524288 | tf_op jit(solution)/shard_map/all_to_all | solution.py:120
  52.6 10.1 %all-to-all-done.1 = f32[8,16,512]{2,1,0:T(8,128)S(1)} async-done(((f32[8,16,512]{2,1,0:T(8,128)}), f32[8,16,512]{2,1,0:T(8,128)S(1)}, u32[]{:S(2)}, u32[]{:S(2)}) %all-to-all-start.1) | async-done | bytes 262176 | tf_op jit(solution)/shard_map/all_to_all | solution.py:120
  62.6 0.1 multiply_reduce_fusion
  62.8 0.0 copy-done.5
  62.8 0.0 copy-done.1
  62.8 0.0 copy-done.7
  62.8 0.0 copy-done.3
  62.8 0.0 copy-done.6
  62.8 3.2 %gated_rows.1 = bf16[4,2,128,512]{3,2,1,0:T(8,128)(2,1)} custom-call(bf16[256,512]{1,0:T(8,128)(2,1)S(1)} %copy-done.6, bf16[256,512]{1,0:T(8,128)(2,1)S(1)} %copy-done.1, bf16[256,512]{1,0:T(8,128)(2,1)S(1)} %copy-done.3, f32[16,512]{1,0:T(8,128)S(1)} %bitcast.27, f32[16,512]{1,0:T(8,128)S(1)} %bitcast.28, f32[16,8,512]{2,1,0:T(8,128)S(1)} %get-tuple-element.7.runs_ref, ...), custom_call_target="tpu_custom_call" | custom-call | tf_op jit(solution)/shard_map/gated_rows/pallas_call | solution.py:106
  66.0 9.4 %all-to-all-start.2 = ((bf16[8,128,512]{2,1,0:T(8,128)(2,1)}), bf16[8,128,512]{2,1,0:T(8,128)(2,1)S(1)}, u32[]{:S(2)}, u32[]{:S(2)}) async-start(bf16[8,128,512]{2,1,0:T(8,128)(2,1)} %bitcast.2), calls=%async_computation.2 | async-start | bytes 2097152 | tf_op jit(solution)/shard_map/all_to_all | solution.py:120
  75.4 0.0 all-gather.2.cloned.1.call-done
  75.4 0.0 copy-start.8
  75.4 2.2 %collective-permute-start.1 = (bf16[1024,512]{1,0:T(8,128)(2,1)}, bf16[1024,512]{1,0:T(8,128)(2,1)S(1)}, u32[]{:S(2)}, u32[]{:S(2)}) collective-permute-start(bf16[1024,512]{1,0:T(8,128)(2,1)} %bitcast.33), channel_id=1, source_target_pairs={{0,1},{1,0},{2,3},{3,2},{4,5},{5,4},{6,7},{7,6},{8,9},{9,8},{10,11... | collective-permute-start | bytes 3145736 | tf_op jit(solution)/shard_map/ppermute | solution.py:116
  77.6 12.9 %all-to-all-done.2 = bf16[8,128,512]{2,1,0:T(8,128)(2,1)S(1)} async-done(((bf16[8,128,512]{2,1,0:T(8,128)(2,1)}), bf16[8,128,512]{2,1,0:T(8,128)(2,1)S(1)}, u32[]{:S(2)}, u32[]{:S(2)}) %all-to-all-start.2) | async-done | bytes 1048608 | tf_op jit(solution)/shard_map/all_to_all | solution.py:120
  90.5 0.1 constant_dynamic-slice_fusion
  90.6 0.0 copy-done.8
  90.6 0.7 fusion.2
  91.3 0.0 collective-permute-done.1
  91.4 0.7 add_convert_fusion
  92.1 32.8 %all_to_all.20 = bf16[16,32,1024]{2,1,0:T(8,128)(2,1)S(1)} all-to-all(bf16[16,32,1024]{2,1,0:T(8,128)(2,1)S(1)} %bitcast.30), channel_id=1, replica_groups=mesh['x'=4,'h'=2,'y'=8,'z'=4,'c'=2] {'x','z'}, dimensions={0} | all-to-all | bytes 2097152 | tf_op jit(solution)/shard_map/all_to_all | solution.py:120
  124.9 0.2 bitcast_reduce_fusion
  125.1 0.7 copy.9
  (5 shorter events, 0.1 us)
Async XLA Ops:
  6.5 56.2 %copy-start.5 = (f32[512,16]{0,1:T(8,128)S(1)}, f32[512,16]{0,1:T(8,128)}, u32[]{:S(2)}) copy-start(f32[512,16]{0,1:T(8,128)} %param.9) | copy-start | bytes 98308
  6.5 56.3 %copy-start.1 = (bf16[256,512]{1,0:T(8,128)(2,1)S(1)}, bf16[256,512]{1,0:T(8,128)(2,1)}, u32[]{:S(2)}) copy-start(bf16[256,512]{1,0:T(8,128)(2,1)} %key_ref.3) | copy-start | bytes 786436
  6.5 56.3 %copy-start.7 = (f32[512,16]{0,1:T(8,128)S(1)}, f32[512,16]{0,1:T(8,128)}, u32[]{:S(2)}) copy-start(f32[512,16]{0,1:T(8,128)} %param.10) | copy-start | bytes 98308
  6.5 68.9 %all-gather.2.cloned.1.call-start = ((), (), s32[]{:S(2)}) async-start(), calls=%async_computation.4 | async-start | bytes 1179648 | tf_op jit(solution)/shard_map/all_gather | solution.py:149
  6.5 13.5 %collective-permute-start = (bf16[64,512]{1,0:T(8,128)(2,1)}, bf16[64,512]{1,0:T(8,128)(2,1)S(1)}, u32[]{:S(2)}, u32[]{:S(2)}) collective-permute-start(bf16[64,512]{1,0:T(8,128)(2,1)} %bitcast.36), channel_id=1, source_target_pairs={{0,64},{64,0},{1,65},{65,1},{2,66},{66,2},{3,67},{67,3},{4,68},{68... | collective-permute-start | bytes 196616 | tf_op jit(solution)/shard_map/ppermute | solution.py:116
  21.7 1.0 copy-start
  22.6 0.9 copy-start.2
  23.6 0.8 copy-start.4
  24.3 38.5 %copy-start.3 = (bf16[256,512]{1,0:T(8,128)(2,1)S(1)}, bf16[256,512]{1,0:T(8,128)(2,1)}, u32[]{:S(2)}) copy-start(bf16[256,512]{1,0:T(8,128)(2,1)} %value_ref.3) | copy-start | bytes 786436
  24.3 38.5 %copy-start.6 = (bf16[256,512]{1,0:T(8,128)(2,1)S(1)}, bf16[256,512]{1,0:T(8,128)(2,1)}, u32[]{:S(2)}) copy-start(bf16[256,512]{1,0:T(8,128)(2,1)} %gate_ref.1) | copy-start | bytes 786436
  26.2 16.2 %all-to-all-start = ((f32[8,16,512]{2,1,0:T(8,128)}), f32[8,16,512]{2,1,0:T(8,128)S(1)}, u32[]{:S(2)}, u32[]{:S(2)}) async-start(f32[8,16,512]{2,1,0:T(8,128)} %broadcast_in_dim.37), calls=%async_computation | async-start | bytes 524288 | tf_op jit(solution)/shard_map/all_to_all | solution.py:120
  43.4 19.3 %all-to-all-start.1 = ((f32[8,16,512]{2,1,0:T(8,128)}), f32[8,16,512]{2,1,0:T(8,128)S(1)}, u32[]{:S(2)}, u32[]{:S(2)}) async-start(f32[8,16,512]{2,1,0:T(8,128)} %broadcast_in_dim.39), calls=%async_computation.1 | async-start | bytes 524288 | tf_op jit(solution)/shard_map/all_to_all | solution.py:120
  66.0 24.5 %all-to-all-start.2 = ((bf16[8,128,512]{2,1,0:T(8,128)(2,1)}), bf16[8,128,512]{2,1,0:T(8,128)(2,1)S(1)}, u32[]{:S(2)}, u32[]{:S(2)}) async-start(bf16[8,128,512]{2,1,0:T(8,128)(2,1)} %bitcast.2), calls=%async_computation.2 | async-start | bytes 2097152 | tf_op jit(solution)/shard_map/all_to_all | solution.py:120
  75.4 15.2 %copy-start.8 = (bf16[8,2,64,512]{3,2,0,1:T(8,128)(2,1)S(1)}, bf16[8,2,64,512]{3,2,0,1:T(8,128)(2,1)}, u32[]{:S(2)}) copy-start(bf16[8,2,64,512]{3,2,0,1:T(8,128)(2,1)} %all-gather.2.cloned.1.call-done) | copy-start | bytes 3145732
  75.4 15.9 %collective-permute-start.1 = (bf16[1024,512]{1,0:T(8,128)(2,1)}, bf16[1024,512]{1,0:T(8,128)(2,1)S(1)}, u32[]{:S(2)}, u32[]{:S(2)}) collective-permute-start(bf16[1024,512]{1,0:T(8,128)(2,1)} %bitcast.33), channel_id=1, source_target_pairs={{0,1},{1,0},{2,3},{3,2},{4,5},{5,4},{6,7},{7,6},{8,9},{9,8},{10,11... | collective-permute-start | bytes 3145736 | tf_op jit(solution)/shard_map/ppermute | solution.py:116
Sparse Core Ops, SparseCore 0:
  21.8 41.5 all-gather.1
where the time goes:
time: 133 us
  starting transfers between devices  39.2 us (29%)
  waiting for transfers between devices  33.5 us (25%)
  blocking collectives  32.8 us (25%)
  between operations  13.6 us (10%)
  local copies, waits for them, and re-layouts  4.92 us (4%)
  Pallas kernels  4.31 us (3%)
  other arithmetic  2.86 us (2%)
  matrix products  1.49 us (1%)
    all_to_all x1, blocking collectives, exchange(): return lax.all_to_all(array, axes, 0, 0, tiled=True)  32.8 us
    all_to_all x3, waiting for transfers between devices, exchange(): return lax.all_to_all(array, axes, 0, 0, tiled=True)  31.6 us
    all_to_all x3, starting transfers between devices, exchange(): return lax.all_to_all(array, axes, 0, 0, tiled=True)  25.4 us
    ppermute x2, starting transfers between devices, swap(): return lax.ppermute(array, axis, [(0, 1), (1, 0)])  13.8 us
    pallas_call x1, Pallas kernels, gated_rows(): pl.pallas_call(gated_kernel, out_shape=jax.ShapeDtypeStruct((NX, NC, leng...  3.15 us
    unnamed x18, local copies, waits for them, and re-layouts  2.67 us
  transfers between devices with their start and end apart: 6, of which 4 were waited for; matrix products, arithmetic and copies ran while one was open for 3% of the time, Pallas kernels for 3%

commit v1 on v0

v1 whole, which is shorter than its diff:
```python
import jax
import jax.numpy as jnp
from jax import lax
from jax.experimental import pallas as pl
from jax.experimental.pallas import tpu as pltpu
from jax.sharding import Mesh, PartitionSpec as P

AXES = (("x", 4), ("h", 2), ("y", 8), ("z", 4), ("c", 2))
NX, NH, NY, NZ, NC = (size for _, size in AXES)
SEQ = ("x", "h", "y")
CH = ("z", "c")
RING = (1, -1, 2)

SUB = 8
LANES = 128
f32 = jnp.float32
bf16 = jnp.bfloat16


def run_states_kernel(key_ref, value_ref, rate_ref, runs_ref, block_ref, signal):
    poles = rate_ref.shape[0]
    steps = key_ref.shape[0] // SUB
    signal[...] = key_ref[...].astype(f32) * value_ref[...].astype(f32)
    later = (SUB - 1 - lax.broadcasted_iota(jnp.int32, (SUB, LANES), 0)).astype(f32) * steps
    rates = [jnp.broadcast_to(rate_ref[pl.ds(r, 1), :], (SUB, LANES)) for r in range(poles)]
    decays = [jnp.exp(-rate) for rate in rates]

    def step(j, states):
        x = signal[pl.ds(j, SUB, stride=steps), :]
        return tuple(d * s + x for d, s in zip(decays, states))

    states = lax.fori_loop(0, steps, step, (jnp.zeros((SUB, LANES), f32),) * poles, unroll=4)
    ends = []
    for r in range(poles):
        runs_ref[r] = states[r]
        ends.append(jnp.sum(states[r] * jnp.exp(-rates[r] * later), axis=0, keepdims=True))
    ends = jnp.concatenate(ends, axis=0).astype(block_ref.dtype)
    for copy in range(block_ref.shape[0]):
        block_ref[copy] = ends


def run_states(key_input, value_input, rate):
    poles, chans = rate.shape
    length = key_input.shape[0]
    return pl.pallas_call(
        run_states_kernel,
        grid=(chans // LANES,),
        in_specs=[
            pl.BlockSpec((length, LANES), lambda i: (0, i)),
            pl.BlockSpec((length, LANES), lambda i: (0, i)),
            pl.BlockSpec((poles, LANES), lambda i: (0, i)),
        ],
        out_specs=(
            pl.BlockSpec((poles, SUB, LANES), lambda i: (0, 0, i)),
            pl.BlockSpec((NY, poles, LANES), lambda i: (0, 0, i)),
        ),
        out_shape=(
            jax.ShapeDtypeStruct((poles, SUB, chans), f32),
            jax.ShapeDtypeStruct((NY, poles, chans), bf16),
        ),
        scratch_shapes=[pltpu.VMEM((length, LANES), f32)],
        compiler_params=pltpu.CompilerParams(vmem_limit_bytes=60 << 20),
        name="run_states",
    )(key_input, value_input, rate)


def gated_kernel(gate_ref, key_ref, value_ref, rate_ref, residue_ref, runs_ref, before_ref, out_ref, signal, conv):
    poles, chans = rate_ref.shape
    steps = key_ref.shape[0] // SUB
    for tile in range(chans // LANES):
        lanes = pl.ds(tile * LANES, LANES)
        signal[tile] = key_ref[:, lanes].astype(f32) * value_ref[:, lanes].astype(f32)
    run = lax.broadcasted_iota(jnp.int32, (SUB, LANES), 0)
    run_f = run.astype(f32)
    for tile in range(chans // LANES):
        lanes = pl.ds(tile * LANES, LANES)
        decays, weights, starts = [], [], []
        for r in range(poles):
            rate = jnp.broadcast_to(rate_ref[pl.ds(r, 1), lanes], (SUB, LANES))
            residue = jnp.broadcast_to(residue_ref[pl.ds(r, 1), lanes], (SUB, LANES))
            before = jnp.broadcast_to(before_ref[pl.ds(r, 1), lanes], (SUB, LANES))
            ends = runs_ref[r, :, lanes]
            for back in (1, 2, 4):
                moved = jnp.where(run >= back, pltpu.roll(ends, back, 0), 0.0)
                ends = ends + jnp.exp(-rate * (steps * back)) * moved
            start = jnp.where(run >= 1, pltpu.roll(ends, 1, 0), 0.0)
            starts.append(start + jnp.exp(-rate * (steps * run_f)) * before)
            decays.append(jnp.exp(-rate))
            weights.append(residue * jnp.sqrt(rate))

        def step(j, states):
            at = pl.ds(j, SUB, stride=steps)
            x = signal[tile, at, :]
            states = tuple(d * s + x for d, s in zip(decays, states))
            terms = [w * s for w, s in zip(weights, states)]
            while len(terms) > 1:
                terms = [a + b for a, b in zip(terms[::2], terms[1::2])]
            conv[tile, at, :] = terms[0]
            return states

        lax.fori_loop(0, steps, step, tuple(starts), unroll=4)
    rows = gate_ref.shape[0] // (NZ * NC)
    for part in range(NZ * NC):
        at = pl.ds(part * rows, rows)
        for tile in range(chans // LANES):
            lanes = pl.ds(tile * LANES, LANES)
            piece = (gate_ref[at, lanes].astype(f32) * conv[tile, at, :]).astype(bf16)
            for copy in range(NX):
                out_ref[part % NC, copy, pl.ds(part // NC * rows, rows), lanes] = piece


def gated_rows(gate_input, key_input, value_input, rate, residue, runs, before):
    length, chans = gate_input.shape
    return pl.pallas_call(
        gated_kernel,
        out_shape=jax.ShapeDtypeStruct((NC, NX, length // NC, chans), bf16),
        scratch_shapes=[pltpu.VMEM((chans // LANES, length, LANES), f32)] * 2,
        compiler_params=pltpu.CompilerParams(vmem_limit_bytes=32 << 20),
        name="gated_rows",
    )(gate_input, key_input, value_input, rate, residue, runs, before)


def project_kernel(order_ref, rows_ref, own_low, own_high, other_low, other_high, out_ref, own, other):
    core = order_ref[0]
    blocks = order_ref.shape[0] - 1
    half = blocks // 2
    width = own_low.shape[0] // half
    for p in range(blocks):
        at = pl.ds(pl.multiple_of(order_ref[1 + p] * width, width), width)
        of = pl.ds(p % half * width, width)
        own[at, :] = (own_low if p < half else own_high)[of, :]
        other[at, :] = (other_low if p < half else other_high)[of, :]
    contract = (((1,), (1,)), ((), ()))
    total = lax.dot_general(rows_ref[core], own[...], contract, preferred_element_type=f32)
    total += lax.dot_general(rows_ref[1 - core], other[...], contract, preferred_element_type=f32)
    out_ref[...] = total.astype(out_ref.dtype)


def project(order, rows, *weights):
    columns, chans = 2 * weights[0].shape[0], weights[0].shape[1]
    return pl.pallas_call(
        project_kernel,
        in_specs=[pl.BlockSpec(memory_space=pltpu.SMEM)] + [pl.BlockSpec(memory_space=pltpu.VMEM)] * 5,
        out_specs=pl.BlockSpec(memory_space=pltpu.VMEM),
        out_shape=jax.ShapeDtypeStruct((rows.shape[1], columns), bf16),
        scratch_shapes=[pltpu.VMEM((columns, chans), bf16)] * 2,
        compiler_params=pltpu.CompilerParams(vmem_limit_bytes=32 << 20),
        name="project",
    )(order, rows, *weights)


def finish_kernel(parts_ref, out_ref):
    columns = parts_ref.shape[-1]
    for x in range(NX):
        total = parts_ref[x, 0].astype(f32)
        for z in range(1, NZ):
            total += parts_ref[x, z].astype(f32)
        out_ref[:, pl.ds(x * columns, columns)] = total.astype(out_ref.dtype)


def finish(parts):
    return pl.pallas_call(
        finish_kernel,
        out_shape=jax.ShapeDtypeStruct((parts.shape[2], NX * parts.shape[3]), bf16),
        compiler_params=pltpu.CompilerParams(vmem_limit_bytes=32 << 20),
        name="finish",
    )(parts)


def swap(array, axis, bit=1):
    return lax.ppermute(array, axis, [(i, i ^ bit) for i in range(dict(AXES)[axis])])


def from_along_y(array, step):
    return lax.ppermute(array, "y", [((i + step) % NY, i) for i in range(NY)])


def with_other(mine, other):
    return jnp.concatenate([mine, other], axis=0)


def exchange(array, axes):
    return lax.all_to_all(array, axes, 0, 0, tiled=True)


def copies(array, count):
    return jnp.broadcast_to(array[None], (count, *array.shape))


def body(gate_input, key_input, value_input, decay_rate, residues, out_weight):
    length, chans = gate_input.shape
    x, h, y, _, core = (lax.axis_index(axis) for axis, _ in AXES)
    rate, residue = decay_rate.T, residues.T

    weight = out_weight.T
    other = swap(weight, "y", 4)

    runs, block = run_states(key_input, value_input, rate)
    other, block = lax.optimization_barrier((other, block))
    weight = with_other(weight, other)
    other = swap(weight, "h", 1)

    blocks = exchange(block, "y")
    blocks = blocks.astype(f32)
    at = jnp.arange(NY)[:, None, None]
    back = y - 1 - at
    inner = jnp.sum(
        jnp.where(back >= 0, jnp.exp(-rate * (length * jnp.maximum(back, 0)).astype(f32)), 0.0) * blocks, axis=0
    )
    total = jnp.sum(jnp.exp(-rate * (length * (NY - 1 - at)).astype(f32)) * blocks, axis=0)
    weight = with_other(weight, other)
    others = tuple(from_along_y(weight, step) for step in RING)
    totals = exchange(copies(total.astype(bf16), NX * NH), ("x", "h"))
    totals = totals.astype(f32)
    back = x * NH + h - 1 - jnp.arange(NX * NH)[:, None, None]
    outer = jnp.sum(
        jnp.where(back >= 0, jnp.exp(-rate * (length * NY * jnp.maximum(back, 0)).astype(f32)), 0.0) * totals, axis=0
    )
    before = inner + jnp.exp(-rate * (length * y).astype(f32)) * outer

    rows = gated_rows(gate_input, key_input, value_input, rate, residue, runs, before)
    arrived = exchange(rows.reshape(NC * NX, length // NC, chans), ("c", "x")).reshape(NC, -1, chans)
    low, high = with_other(weight, others[0]), with_other(others[1], others[2])
    weights = (low, high, swap(low, "c", 1), swap(high, "c", 1))

    steps, a, b = jnp.array((0, *RING))[:, None, None], jnp.arange(2), jnp.arange(2)[:, None]
    place = ((h ^ b) * NY + ((y + steps) % NY ^ (4 * a))).reshape(-1)
    order = jnp.concatenate([core[None], place]).astype(jnp.int32)
    partial = project(order, arrived, *weights)
    columns = partial.shape[1]
    parts = exchange(partial.reshape(NX * NZ, -1, columns), ("x", "z"))
    return finish(parts.reshape(NX, NZ, -1, columns))


def solution(mesh):
    names, sizes = zip(*AXES)
    fine = Mesh(mesh.devices.reshape(sizes), names)
    return jax.shard_map(
        body,
        mesh=fine,
        in_specs=(P(SEQ, CH), P(SEQ, CH), P(SEQ, CH), P(CH, None), P(CH, None), P(CH, SEQ)),
        out_specs=P(SEQ + CH, None),
        check_vma=False,
    )
```

time: 133 us -> 112 us (0.84)
  waiting for transfers between devices: 33.5 us -> 9.93 us
  starting transfers between devices: 39.2 us -> 56.4 us
  between operations: 13.6 us -> 0.33 us
  Pallas kernels: 4.31 us -> 9.44 us
  local copies, waits for them, and re-layouts: 4.92 us -> 2.15 us
  other arithmetic: 2.86 us -> 0.68 us
  matrix products: 1.49 us -> 0 us
    all_to_all x3, waiting for transfers between devices: 31.6 us -> 8.72 us  [exchange(): return lax.all_to_all(array, axes, 0, 0, tiled=True)]
    ppermute x2 -> x7, starting transfers between devices: 13.8 us -> 31.6 us  [the longest x4 23 us: swap(): lax.ppermute(array, axis, [(i, i ^ bit) for i in range(dict(AXES)[axis])])]
    pallas_call x2 -> x4, Pallas kernels: 4.31 us -> 9.44 us  [the longest x1 3.6 us: run_states(): pl.pallas_call(run_states_kernel, grid=(chans // LANES,), in_specs=[pl.Bl...]
    select_n x1, other arithmetic: 1.57 us -> 0.01 us  [body(): place = ((h ^ b) * NY + ((y + steps) % NY ^ 4 * a)).reshape(-1)]
    dot_general x2 -> x0, matrix products: 1.49 us -> none  [the longest x1 0.75 us: body(): lax.dot_general(other, other_weight, contract, preferred_element_type=f32)]
    unnamed x18 -> x19, local copies, waits for them, and re-layouts: 2.67 us -> 1.38 us
  transfers between devices with their start and end apart: 6 -> 10, of which waited for: 4 -> 3; matrix products, arithmetic and copies ran while one was open for 3% -> 1% of each run, Pallas kernels for 3% -> 6%
where the time goes in v1:
time: 112 us; the launch traced here: 111 us
  starting transfers between devices  56.4 us (50%)
  blocking collectives  31.8 us (28%)
  waiting for transfers between devices  9.93 us (9%)
  Pallas kernels  9.44 us (8%)
  local copies, waits for them, and re-layouts  2.15 us (2%)
    all_to_all x1, blocking collectives, exchange(): return lax.all_to_all(array, axes, 0, 0, tiled=True)  31.8 us
    all_to_all x3, starting transfers between devices, exchange(): return lax.all_to_all(array, axes, 0, 0, tiled=True)  24.9 us
    ppermute x4, starting transfers between devices, swap(): lax.ppermute(array, axis, [(i, i ^ bit) for i in range(dict(AXES)[axis])])  23 us
    all_to_all x3, waiting for transfers between devices, exchange(): return lax.all_to_all(array, axes, 0, 0, tiled=True)  8.72 us
    ppermute x3, starting transfers between devices, from_along_y(): return lax.ppermute(array, 'y', [((i + step) % NY, i) for i in range(NY)])  8.55 us
    pallas_call x1, Pallas kernels, run_states(): pl.pallas_call(run_states_kernel, grid=(chans // LANES,), in_specs=[pl.Bl...  3.6 us
    pallas_call x1, Pallas kernels, gated_rows(): pl.pallas_call(gated_kernel, out_shape=jax.ShapeDtypeStruct((NC, NX, leng...  3.12 us
  transfers between devices with their start and end apart: 10, of which 3 were waited for; matrix products, arithmetic and copies ran while one was open for 1% of the time, Pallas kernels for 6%

profile of v1, /device:TPU:1, one launch (start us, length us, event | category | flops | bytes accessed | tf_op | source)
XLA Modules:
  0.0 110.8 jit_solution(5548965205853797938)
XLA Ops:
  0.0 0.0 copy-start.2
  0.0 8.4 %collective-permute-start = (bf16[64,512]{1,0:T(8,128)(2,1)}, bf16[64,512]{1,0:T(8,128)(2,1)S(1)}, u32[]{:S(2)}, u32[]{:S(2)}) collective-permute-start(bf16[64,512]{1,0:T(8,128)(2,1)} %bitcast.17), channel_id=1, source_target_pairs={{0,32},{8,40},{16,48},{24,56},{32,0},{40,8},{48,16},{56,24},{1,33}... | collective-permute-start | bytes 196616 | tf_op jit(solution)/shard_map/ppermute | solution.py:171
  8.5 0.0 copy-done.2
  8.5 0.0 copy-start.8
  8.5 0.6 copy-done.8
  9.1 3.6 %run_states.1 = (f32[16,8,512]{2,1,0:T(8,128)}, bf16[8,16,512]{2,1,0:T(8,128)(2,1)}) custom-call(bf16[256,512]{1,0:T(8,128)(2,1)} %key_ref.3, bf16[256,512]{1,0:T(8,128)(2,1)} %value_ref.3, f32[16,512]{1,0:T(8,128)} %bitcast.14), custom_call_target="tpu_custom_call" | custom-call | tf_op jit(solution)/shard_map/run_states/pallas_call | solution.py:45
  12.7 0.0 collective-permute-done
  12.7 0.0 copy-start.7
  12.8 6.1 %all-to-all-start = ((bf16[8,16,512]{2,1,0:T(8,128)(2,1)}), bf16[8,16,512]{2,1,0:T(8,128)(2,1)S(1)}, u32[]{:S(2)}, u32[]{:S(2)}) async-start(bf16[8,16,512]{2,1,0:T(8,128)(2,1)} %get-tuple-element.11), calls=%async_computation | async-start | bytes 262144 | tf_op jit(solution)/shard_map/all_to_all | solution.py:183
  18.9 0.0 copy-done.7
  18.9 9.1 %collective-permute-start.1 = (bf16[128,512]{1,0:T(8,128)(2,1)S(1)}, bf16[128,512]{1,0:T(8,128)(2,1)S(1)}, u32[]{:S(2)}, u32[]{:S(2)}) collective-permute-start(bf16[128,512]{1,0:T(8,128)(2,1)S(1)} %pad_maximum_fusion.2), channel_id=1, source_target_pairs={{0,64},{64,0},{1,65},{65,1},{2,66},{66,2},{3,67},{67,3},{4,68},{68... | collective-permute-start | bytes 393224 | tf_op jit(solution)/shard_map/ppermute | solution.py:171
  28.0 0.0 all-to-all-done
  28.0 0.2 fusion.1
  28.2 0.7 broadcast_in_dim.40
  28.9 0.0 copy-start.5
  28.9 9.9 %all-to-all-start.1 = ((bf16[8,16,512]{2,1,0:T(8,128)(2,1)}), bf16[8,16,512]{2,1,0:T(8,128)(2,1)S(1)}, u32[]{:S(2)}, u32[]{:S(2)}) async-start(bf16[8,16,512]{2,1,0:T(8,128)(2,1)} %broadcast_in_dim.40), calls=%async_computation.1 | async-start | bytes 262144 | tf_op jit(solution)/shard_map/all_to_all | solution.py:183
  38.8 0.0 collective-permute-done.1
  38.8 0.0 copy-start.3
  38.8 0.0 copy-start.1
  38.8 0.0 copy-start.4
  38.8 0.0 copy-start
  38.8 2.2 %collective-permute-start.3 = (bf16[256,512]{1,0:T(8,128)(2,1)S(1)}, bf16[256,512]{1,0:T(8,128)(2,1)S(1)}, u32[]{:S(2)}, u32[]{:S(2)}) collective-permute-start(bf16[256,512]{1,0:T(8,128)(2,1)S(1)} %pad_maximum_fusion.1), channel_id=1, source_target_pairs={{56,0},{0,8},{8,16},{16,24},{24,32},{32,40},{40,48},{48,56},{57,1}... | collective-permute-start | bytes 786440 | tf_op jit(solution)/shard_map/ppermute | solution.py:175
  41.1 2.5 %collective-permute-start.4 = (bf16[256,512]{1,0:T(8,128)(2,1)S(1)}, bf16[256,512]{1,0:T(8,128)(2,1)S(1)}, u32[]{:S(2)}, u32[]{:S(2)}) collective-permute-start(bf16[256,512]{1,0:T(8,128)(2,1)S(1)} %pad_maximum_fusion.1), channel_id=1, source_target_pairs={{16,0},{24,8},{32,16},{40,24},{48,32},{56,40},{0,48},{8,56},{17,1}... | collective-permute-start | bytes 786440 | tf_op jit(solution)/shard_map/ppermute | solution.py:175
  43.6 3.8 %collective-permute-start.2 = (bf16[256,512]{1,0:T(8,128)(2,1)S(1)}, bf16[256,512]{1,0:T(8,128)(2,1)S(1)}, u32[]{:S(2)}, u32[]{:S(2)}) collective-permute-start(bf16[256,512]{1,0:T(8,128)(2,1)S(1)} %pad_maximum_fusion.1), channel_id=1, source_target_pairs={{8,0},{16,8},{24,16},{32,24},{40,32},{48,40},{56,48},{0,56},{9,1},... | collective-permute-start | bytes 786440 | tf_op jit(solution)/shard_map/ppermute | solution.py:175
  47.4 0.9 all-to-all-done.1
  48.3 0.1 multiply_reduce_fusion
  48.5 0.0 copy-done.3
  48.5 0.0 copy-start.6
  48.5 0.0 copy-done.5
  48.5 0.0 copy-done.1
  48.5 0.0 copy-done.4
  48.5 0.0 copy-done
  48.6 0.7 copy-done.6
  49.2 3.1 %gated_rows.1 = bf16[2,4,128,512]{3,2,1,0:T(8,128)(2,1)} custom-call(bf16[256,512]{1,0:T(8,128)(2,1)S(1)} %copy-done.4, bf16[256,512]{1,0:T(8,128)(2,1)S(1)} %copy-done, bf16[256,512]{1,0:T(8,128)(2,1)S(1)} %copy-done.1, f32[16,512]{1,0:T(8,128)S(1)} %bitcast.15, f32[16,512]{1,0:T(8,128)S(1)} %bitcast.16, f32[16,8,512]{2,1,0:T(8,128)S(1)} %copy-done.5, ...), custom_call_target="tpu_custom_call" | custom-call | tf_op jit(solution)/shard_map/gated_rows/pallas_call | solution.py:114
  52.4 8.9 %all-to-all-start.2 = ((bf16[8,128,512]{2,1,0:T(8,128)(2,1)}), bf16[8,128,512]{2,1,0:T(8,128)(2,1)S(1)}, u32[]{:S(2)}, u32[]{:S(2)}) async-start(bf16[8,128,512]{2,1,0:T(8,128)(2,1)} %bitcast.4), calls=%async_computation.2 | async-start | bytes 2097152 | tf_op jit(solution)/shard_map/all_to_all | solution.py:183
  61.3 0.0 collective-permute-done.3
  61.3 0.0 collective-permute-done.4
  61.3 2.0 %collective-permute-start.6 = (bf16[512,512]{1,0:T(8,128)(2,1)S(1)}, bf16[512,512]{1,0:T(8,128)(2,1)S(1)}, u32[]{:S(2)}, u32[]{:S(2)}) collective-permute-start(bf16[512,512]{1,0:T(8,128)(2,1)S(1)} %constant_dynamic-update-slice_fusion.own_high), channel_id=1, source_target_pairs={{0,1},{1,0},{2,3},{3,2},{4,5},{5,4},{6,7},{7,6},{8,9},{9,8},{10,11... | collective-permute-start | bytes 1572872 | tf_op jit(solution)/shard_map/ppermute | solution.py:171
  63.3 0.0 collective-permute-done.2
  63.4 3.5 %collective-permute-start.5 = (bf16[512,512]{1,0:T(8,128)(2,1)S(1)}, bf16[512,512]{1,0:T(8,128)(2,1)S(1)}, u32[]{:S(2)}, u32[]{:S(2)}) collective-permute-start(bf16[512,512]{1,0:T(8,128)(2,1)S(1)} %pad_maximum_fusion.own_low), channel_id=1, source_target_pairs={{0,1},{1,0},{2,3},{3,2},{4,5},{5,4},{6,7},{7,6},{8,9},{9,8},{10,11... | collective-permute-start | bytes 1572872 | tf_op jit(solution)/shard_map/ppermute | solution.py:171
  66.9 0.1 broadcast_xor_fusion
  67.0 0.1 broadcast_add_fusion
  67.1 0.1 add.45
  67.2 0.1 pad_add_fusion.order_ref
  67.3 0.0 collective-permute-done.6.other_high
  67.3 1.2 %collective-permute-done.5.other_low = bf16[512,512]{1,0:T(8,128)(2,1)S(1)} collective-permute-done((bf16[512,512]{1,0:T(8,128)(2,1)S(1)}, bf16[512,512]{1,0:T(8,128)(2,1)S(1)}, u32[]{:S(2)}, u32[]{:S(2)}) %collective-permute-start.5) | collective-permute-done | bytes 524320 | tf_op jit(solution)/shard_map/ppermute | solution.py:171
  68.5 7.8 %all-to-all-done.2 = bf16[8,128,512]{2,1,0:T(8,128)(2,1)S(1)} async-done(((bf16[8,128,512]{2,1,0:T(8,128)(2,1)}), bf16[8,128,512]{2,1,0:T(8,128)(2,1)S(1)}, u32[]{:S(2)}, u32[]{:S(2)}) %all-to-all-start.2) | async-done | bytes 1048608 | tf_op jit(solution)/shard_map/all_to_all | solution.py:183
  76.3 1.9 %project.1 = bf16[512,1024]{1,0:T(8,128)(2,1)S(1)} custom-call(s32[17]{0:T(128)S(1)} %pad_add_fusion.order_ref, bf16[2,512,512]{2,1,0:T(8,128)(2,1)S(1)} %bitcast.11, bf16[512,512]{1,0:T(8,128)(2,1)S(1)} %pad_maximum_fusion.own_low, bf16[512,512]{1,0:T(8,128)(2,1)S(1)} %constant_dynamic-update-slice_fusion.own_high, ...), custom_call_target="tpu_custom_call" | custom-call | tf_op jit(solution)/shard_map/project/pallas_call | solution.py:141
  78.2 31.8 %all_to_all.20 = bf16[16,32,1024]{2,1,0:T(8,128)(2,1)S(1)} all-to-all(bf16[16,32,1024]{2,1,0:T(8,128)(2,1)S(1)} %bitcast.12), channel_id=1, replica_groups=mesh['x'=4,'h'=2,'y'=8,'z'=4,'c'=2] {'x','z'}, dimensions={0} | all-to-all | bytes 2097152 | tf_op jit(solution)/shard_map/all_to_all | solution.py:183
  110.0 0.8 finish.1
  (14 shorter events, 0.2 us)
Async XLA Ops:
  0.0 8.5 %copy-start.2 = (f32[512,16]{0,1:T(8,128)S(1)}, f32[512,16]{0,1:T(8,128)}, u32[]{:S(2)}) copy-start(f32[512,16]{0,1:T(8,128)} %param.10) | copy-start | bytes 98308
  0.0 12.7 %collective-permute-start = (bf16[64,512]{1,0:T(8,128)(2,1)}, bf16[64,512]{1,0:T(8,128)(2,1)S(1)}, u32[]{:S(2)}, u32[]{:S(2)}) collective-permute-start(bf16[64,512]{1,0:T(8,128)(2,1)} %bitcast.17), channel_id=1, source_target_pairs={{0,32},{8,40},{16,48},{24,56},{32,0},{40,8},{48,16},{56,24},{1,33}... | collective-permute-start | bytes 196616 | tf_op jit(solution)/shard_map/ppermute | solution.py:171
  8.5 0.7 copy-start.8
  12.7 6.1 %copy-start.7 = (bf16[512,64]{0,1:T(8,128)(2,1)S(1)}, bf16[512,64]{0,1:T(8,128)(2,1)}, u32[]{:S(2)}) copy-start(bf16[512,64]{0,1:T(8,128)(2,1)} %param.12) | copy-start | bytes 196612
  12.8 15.2 %all-to-all-start = ((bf16[8,16,512]{2,1,0:T(8,128)(2,1)}), bf16[8,16,512]{2,1,0:T(8,128)(2,1)S(1)}, u32[]{:S(2)}, u32[]{:S(2)}) async-start(bf16[8,16,512]{2,1,0:T(8,128)(2,1)} %get-tuple-element.11), calls=%async_computation | async-start | bytes 262144 | tf_op jit(solution)/shard_map/all_to_all | solution.py:183
  18.9 19.9 %collective-permute-start.1 = (bf16[128,512]{1,0:T(8,128)(2,1)S(1)}, bf16[128,512]{1,0:T(8,128)(2,1)S(1)}, u32[]{:S(2)}, u32[]{:S(2)}) collective-permute-start(bf16[128,512]{1,0:T(8,128)(2,1)S(1)} %pad_maximum_fusion.2), channel_id=1, source_target_pairs={{0,64},{64,0},{1,65},{65,1},{2,66},{66,2},{3,67},{67,3},{4,68},{68... | collective-permute-start | bytes 393224 | tf_op jit(solution)/shard_map/ppermute | solution.py:171
  28.9 19.7 %copy-start.5 = (f32[16,8,512]{2,1,0:T(8,128)S(1)}, f32[16,8,512]{2,1,0:T(8,128)}, u32[]{:S(2)}) copy-start(f32[16,8,512]{2,1,0:T(8,128)} %get-tuple-element.9.runs_ref) | copy-start | bytes 786436
  28.9 19.5 %all-to-all-start.1 = ((bf16[8,16,512]{2,1,0:T(8,128)(2,1)}), bf16[8,16,512]{2,1,0:T(8,128)(2,1)S(1)}, u32[]{:S(2)}, u32[]{:S(2)}) async-start(bf16[8,16,512]{2,1,0:T(8,128)(2,1)} %broadcast_in_dim.40), calls=%async_computation.1 | async-start | bytes 262144 | tf_op jit(solution)/shard_map/all_to_all | solution.py:183
  38.8 9.7 %copy-start.3 = (f32[512,16]{0,1:T(8,128)S(1)}, f32[512,16]{0,1:T(8,128)}, u32[]{:S(2)}) copy-start(f32[512,16]{0,1:T(8,128)} %param.10) | copy-start | bytes 98308
  38.8 9.7 %copy-start.1 = (bf16[256,512]{1,0:T(8,128)(2,1)S(1)}, bf16[256,512]{1,0:T(8,128)(2,1)}, u32[]{:S(2)}) copy-start(bf16[256,512]{1,0:T(8,128)(2,1)} %value_ref.3) | copy-start | bytes 786436
  38.8 9.7 %copy-start.4 = (bf16[256,512]{1,0:T(8,128)(2,1)S(1)}, bf16[256,512]{1,0:T(8,128)(2,1)}, u32[]{:S(2)}) copy-start(bf16[256,512]{1,0:T(8,128)(2,1)} %gate_ref.1) | copy-start | bytes 786436
  38.8 9.7 %copy-start = (bf16[256,512]{1,0:T(8,128)(2,1)S(1)}, bf16[256,512]{1,0:T(8,128)(2,1)}, u32[]{:S(2)}) copy-start(bf16[256,512]{1,0:T(8,128)(2,1)} %key_ref.3) | copy-start | bytes 786436
  38.8 22.4 %collective-permute-start.3 = (bf16[256,512]{1,0:T(8,128)(2,1)S(1)}, bf16[256,512]{1,0:T(8,128)(2,1)S(1)}, u32[]{:S(2)}, u32[]{:S(2)}) collective-permute-start(bf16[256,512]{1,0:T(8,128)(2,1)S(1)} %pad_maximum_fusion.1), channel_id=1, source_target_pairs={{56,0},{0,8},{8,16},{16,24},{24,32},{32,40},{40,48},{48,56},{57,1}... | collective-permute-start | bytes 786440 | tf_op jit(solution)/shard_map/ppermute | solution.py:175
  41.1 20.2 %collective-permute-start.4 = (bf16[256,512]{1,0:T(8,128)(2,1)S(1)}, bf16[256,512]{1,0:T(8,128)(2,1)S(1)}, u32[]{:S(2)}, u32[]{:S(2)}) collective-permute-start(bf16[256,512]{1,0:T(8,128)(2,1)S(1)} %pad_maximum_fusion.1), channel_id=1, source_target_pairs={{16,0},{24,8},{32,16},{40,24},{48,32},{56,40},{0,48},{8,56},{17,1}... | collective-permute-start | bytes 786440 | tf_op jit(solution)/shard_map/ppermute | solution.py:175
  43.6 19.8 %collective-permute-start.2 = (bf16[256,512]{1,0:T(8,128)(2,1)S(1)}, bf16[256,512]{1,0:T(8,128)(2,1)S(1)}, u32[]{:S(2)}, u32[]{:S(2)}) collective-permute-start(bf16[256,512]{1,0:T(8,128)(2,1)S(1)} %pad_maximum_fusion.1), channel_id=1, source_target_pairs={{8,0},{16,8},{24,16},{32,24},{40,32},{48,40},{56,48},{0,56},{9,1},... | collective-permute-start | bytes 786440 | tf_op jit(solution)/shard_map/ppermute | solution.py:175
  48.5 0.8 copy-start.6
  52.4 23.9 %all-to-all-start.2 = ((bf16[8,128,512]{2,1,0:T(8,128)(2,1)}), bf16[8,128,512]{2,1,0:T(8,128)(2,1)S(1)}, u32[]{:S(2)}, u32[]{:S(2)}) async-start(bf16[8,128,512]{2,1,0:T(8,128)(2,1)} %bitcast.4), calls=%async_computation.2 | async-start | bytes 2097152 | tf_op jit(solution)/shard_map/all_to_all | solution.py:183
  61.3 5.9 %collective-permute-start.6 = (bf16[512,512]{1,0:T(8,128)(2,1)S(1)}, bf16[512,512]{1,0:T(8,128)(2,1)S(1)}, u32[]{:S(2)}, u32[]{:S(2)}) collective-permute-start(bf16[512,512]{1,0:T(8,128)(2,1)S(1)} %constant_dynamic-update-slice_fusion.own_high), channel_id=1, source_target_pairs={{0,1},{1,0},{2,3},{3,2},{4,5},{5,4},{6,7},{7,6},{8,9},{9,8},{10,11... | collective-permute-start | bytes 1572872 | tf_op jit(solution)/shard_map/ppermute | solution.py:171
  63.4 5.1 %collective-permute-start.5 = (bf16[512,512]{1,0:T(8,128)(2,1)S(1)}, bf16[512,512]{1,0:T(8,128)(2,1)S(1)}, u32[]{:S(2)}, u32[]{:S(2)}) collective-permute-start(bf16[512,512]{1,0:T(8,128)(2,1)S(1)} %pad_maximum_fusion.own_low), channel_id=1, source_target_pairs={{0,1},{1,0},{2,3},{3,2},{4,5},{5,4},{6,7},{7,6},{8,9},{9,8},{10,11... | collective-permute-start | bytes 1572872 | tf_op jit(solution)/shard_map/ppermute | solution.py:171

commit v2 on v1

v2 whole, which is shorter than its diff:
```python
import jax
import jax.numpy as jnp
from jax import lax
from jax.experimental import pallas as pl
from jax.experimental.pallas import tpu as pltpu
from jax.sharding import Mesh, PartitionSpec as P

AXES = (("x", 4), ("h", 2), ("y", 8), ("z", 4), ("c", 2))
NX, NH, NY, NZ, NC = (size for _, size in AXES)
SEQ = ("x", "h", "y")
CH = ("z", "c")
RING = (2, 1, -1)

SUB = 8
LANES = 128
f32 = jnp.float32
bf16 = jnp.bfloat16


def run_states_kernel(key_ref, value_ref, rate_ref, residue_ref, runs_ref, block_ref, weight_ref, signal):
    weight_ref[...] = residue_ref[...] * jnp.sqrt(rate_ref[...])
    poles, chans = rate_ref.shape
    steps = key_ref.shape[0] // SUB
    later = (SUB - 1 - lax.broadcasted_iota(jnp.int32, (SUB, LANES), 0)).astype(f32) * steps
    for tile in range(chans // LANES):
        lanes = pl.ds(tile * LANES, LANES)
        signal[...] = key_ref[:, lanes].astype(f32) * value_ref[:, lanes].astype(f32)
        rates = [jnp.broadcast_to(rate_ref[pl.ds(r, 1), lanes], (SUB, LANES)) for r in range(poles)]
        decays = [jnp.exp(-rate) for rate in rates]

        def step(j, states):
            x = signal[pl.ds(j, SUB, stride=steps), :]
            return tuple(d * s + x for d, s in zip(decays, states))

        states = lax.fori_loop(0, steps, step, (jnp.zeros((SUB, LANES), f32),) * poles, unroll=8)
        ends = []
        for r in range(poles):
            runs_ref[r, :, lanes] = states[r]
            ends.append(jnp.sum(states[r] * jnp.exp(-rates[r] * later), axis=0, keepdims=True))
        ends = jnp.concatenate(ends, axis=0).astype(block_ref.dtype)
        for copy in range(block_ref.shape[0]):
            block_ref[copy, :, lanes] = ends


def run_states(key_input, value_input, rate, residue):
    poles, chans = rate.shape
    return pl.pallas_call(
        run_states_kernel,
        out_shape=(
            jax.ShapeDtypeStruct((poles, SUB, chans), f32),
            jax.ShapeDtypeStruct((NY, poles, chans), bf16),
            jax.ShapeDtypeStruct((poles, chans), f32),
        ),
        scratch_shapes=[pltpu.VMEM((key_input.shape[0], LANES), f32)],
        compiler_params=pltpu.CompilerParams(vmem_limit_bytes=60 << 20),
        name="run_states",
    )(key_input, value_input, rate, residue)


def gated_kernel(gate_ref, key_ref, value_ref, rate_ref, weight_ref, runs_ref, before_ref, out_ref, signal, conv):
    poles, chans = rate_ref.shape
    steps = key_ref.shape[0] // SUB
    for tile in range(chans // LANES):
        lanes = pl.ds(tile * LANES, LANES)
        signal[tile] = key_ref[:, lanes].astype(f32) * value_ref[:, lanes].astype(f32)
    run = lax.broadcasted_iota(jnp.int32, (SUB, LANES), 0)
    run_f = run.astype(f32)
    for tile in range(chans // LANES):
        lanes = pl.ds(tile * LANES, LANES)
        decays, weights, starts = [], [], []
        for r in range(poles):
            rate = jnp.broadcast_to(rate_ref[pl.ds(r, 1), lanes], (SUB, LANES))
            before = jnp.broadcast_to(before_ref[pl.ds(r, 1), lanes], (SUB, LANES))
            ends = runs_ref[r, :, lanes]
            for back in (1, 2, 4):
                moved = jnp.where(run >= back, pltpu.roll(ends, back, 0), 0.0)
                ends = ends + jnp.exp(-rate * (steps * back)) * moved
            start = jnp.where(run >= 1, pltpu.roll(ends, 1, 0), 0.0)
            starts.append(start + jnp.exp(-rate * (steps * run_f)) * before)
            decays.append(jnp.exp(-rate))
            weights.append(jnp.broadcast_to(weight_ref[pl.ds(r, 1), lanes], (SUB, LANES)))

        def step(j, states):
            at = pl.ds(j, SUB, stride=steps)
            x = signal[tile, at, :]
            states = tuple(d * s + x for d, s in zip(decays, states))
            terms = [w * s for w, s in zip(weights, states)]
            while len(terms) > 1:
                terms = [a + b for a, b in zip(terms[::2], terms[1::2])]
            conv[tile, at, :] = terms[0]
            return states

        lax.fori_loop(0, steps, step, tuple(starts), unroll=True)
    rows = gate_ref.shape[0] // (NZ * NC)
    for part in range(NZ * NC):
        at = pl.ds(part * rows, rows)
        for tile in range(chans // LANES):
            lanes = pl.ds(tile * LANES, LANES)
            piece = (gate_ref[at, lanes].astype(f32) * conv[tile, at, :]).astype(bf16)
            for copy in range(NX):
                out_ref[part % NC, copy, pl.ds(part // NC * rows, rows), lanes] = piece


def gated_rows(gate_input, key_input, value_input, rate, pole_weight, runs, before):
    length, chans = gate_input.shape
    return pl.pallas_call(
        gated_kernel,
        out_shape=jax.ShapeDtypeStruct((NC, NX, length // NC, chans), bf16),
        scratch_shapes=[pltpu.VMEM((chans // LANES, length, LANES), f32)] * 2,
        compiler_params=pltpu.CompilerParams(vmem_limit_bytes=32 << 20),
        name="gated_rows",
    )(gate_input, key_input, value_input, rate, pole_weight, runs, before)


def project_kernel(place_ref, rows_ref, own_low, own_high, other_low, other_high, out_ref, own, other):
    h, y, core = place_ref[0], place_ref[1], place_ref[2]
    blocks = NH * NY
    half = blocks // 2
    width = own_low.shape[0] // half
    for p in range(blocks):
        step, b, a = (0, *RING)[p // 4], p // 2 % 2, p % 2
        block = (h + b) % NH * NY + (y + step + 4 * a + NY) % NY
        at = pl.ds(pl.multiple_of(block * width, width), width)
        of = pl.ds(p % half * width, width)
        own[at, :] = (own_low if p < half else own_high)[of, :]
        other[at, :] = (other_low if p < half else other_high)[of, :]
    contract = (((1,), (1,)), ((), ()))
    total = lax.dot_general(rows_ref[core], own[...], contract, preferred_element_type=f32)
    total += lax.dot_general(rows_ref[1 - core], other[...], contract, preferred_element_type=f32)
    rows = out_ref.shape[2]
    for x in range(NX):
        for z in range(NZ):
            out_ref[z, x] = total[(x * NZ + z) * rows : (x * NZ + z + 1) * rows].astype(out_ref.dtype)


def project(place, rows, *weights):
    columns, chans = 2 * weights[0].shape[0], weights[0].shape[1]
    return pl.pallas_call(
        project_kernel,
        in_specs=[pl.BlockSpec(memory_space=pltpu.SMEM)] + [pl.BlockSpec(memory_space=pltpu.VMEM)] * 5,
        out_specs=pl.BlockSpec(memory_space=pltpu.VMEM),
        out_shape=jax.ShapeDtypeStruct((NZ, NX, rows.shape[1] // (NZ * NX), columns), bf16),
        scratch_shapes=[pltpu.VMEM((columns, chans), bf16)] * 2,
        compiler_params=pltpu.CompilerParams(vmem_limit_bytes=32 << 20),
        name="project",
    )(place, rows, *weights)


def finish_kernel(parts_ref, out_ref):
    columns = parts_ref.shape[-1]
    for x in range(NX):
        total = parts_ref[0, x].astype(f32)
        for z in range(1, NZ):
            total += parts_ref[z, x].astype(f32)
        out_ref[:, pl.ds(x * columns, columns)] = total.astype(out_ref.dtype)


def finish(parts):
    return pl.pallas_call(
        finish_kernel,
        out_shape=jax.ShapeDtypeStruct((parts.shape[2], NX * parts.shape[3]), bf16),
        compiler_params=pltpu.CompilerParams(vmem_limit_bytes=32 << 20),
        name="finish",
    )(parts)


def swap(array, axis, bit=1):
    return lax.ppermute(array, axis, [(i, i ^ bit) for i in range(dict(AXES)[axis])])


def from_along_y(array, step):
    return lax.ppermute(array, "y", [((i + step) % NY, i) for i in range(NY)])


def with_other(mine, other):
    return jnp.concatenate([mine, other], axis=0)


def exchange(array, axes):
    return lax.all_to_all(array, axes, 0, 0, tiled=True)


def copies(array, count):
    return jnp.broadcast_to(array[None], (count, *array.shape))


def body(gate_input, key_input, value_input, decay_rate, residues, out_weight):
    length, chans = gate_input.shape
    x, h, y, _, core = (lax.axis_index(axis) for axis, _ in AXES)
    rate, residue = decay_rate.T, residues.T

    weight = out_weight.T
    other = swap(weight, "y", 4)

    runs, block, pole_weight = run_states(key_input, value_input, rate, residue)
    weight = with_other(weight, other)
    other = swap(weight, "h", 1)

    blocks = exchange(block, "y")
    blocks = blocks.astype(f32)
    at = jnp.arange(NY)[:, None, None]
    back = y - 1 - at
    inner = jnp.sum(
        jnp.where(back >= 0, jnp.exp(-rate * (length * jnp.maximum(back, 0)).astype(f32)), 0.0) * blocks, axis=0
    )
    total = jnp.sum(jnp.exp(-rate * (length * (NY - 1 - at)).astype(f32)) * blocks, axis=0)
    weight = with_other(weight, other)
    others = [from_along_y(weight, step) for step in RING[:2]]
    totals = exchange(copies(total.astype(bf16), NX * NH), ("x", "h"))
    totals = totals.astype(f32)
    back = x * NH + h - 1 - jnp.arange(NX * NH)[:, None, None]
    outer = jnp.sum(
        jnp.where(back >= 0, jnp.exp(-rate * (length * NY * jnp.maximum(back, 0)).astype(f32)), 0.0) * totals, axis=0
    )
    before = inner + jnp.exp(-rate * (length * y).astype(f32)) * outer

    rows = gated_rows(gate_input, key_input, value_input, rate, pole_weight, runs, before)
    late, rows = lax.optimization_barrier((weight, rows))
    others.append(from_along_y(late, RING[2]))
    arrived = exchange(rows.reshape(NC * NX, length // NC, chans), ("c", "x")).reshape(NC, -1, chans)
    low, high = with_other(weight, others[0]), with_other(others[1], others[2])
    weights = (low, high, swap(low, "c", 1), swap(high, "c", 1))

    place = jnp.stack([h, y, core]).astype(jnp.int32)
    partial = project(place, arrived, *weights)
    columns = partial.shape[-1]
    parts = exchange(partial.reshape(NZ * NX, -1, columns), ("z", "x"))
    return finish(parts.reshape(NZ, NX, -1, columns))


def solution(mesh):
    names, sizes = zip(*AXES)
    fine = Mesh(mesh.devices.reshape(sizes), names)
    return jax.shard_map(
        body,
        mesh=fine,
        in_specs=(P(SEQ, CH), P(SEQ, CH), P(SEQ, CH), P(CH, None), P(CH, None), P(CH, SEQ)),
        out_specs=P(SEQ + CH, None),
        check_vma=False,
    )
```

time: 112 us -> 107 us (0.955)
  starting transfers between devices: 56.4 us -> 49.9 us
  waiting for transfers between devices: 9.93 us -> 12.9 us
    ppermute x3, waiting for transfers between devices: 0.01 us -> 6.74 us  [from_along_y(): return lax.ppermute(array, 'y', [((i + step) % NY, i) for i in range(NY)])]
    all_to_all x3, starting transfers between devices: 24.9 us -> 19.4 us  [exchange(): return lax.all_to_all(array, axes, 0, 0, tiled=True)]
    all_to_all x3, waiting for transfers between devices: 8.72 us -> 4.77 us  [exchange(): return lax.all_to_all(array, axes, 0, 0, tiled=True)]
    ppermute x3, starting transfers between devices: 8.55 us -> 6.53 us  [from_along_y(): return lax.ppermute(array, 'y', [((i + step) % NY, i) for i in range(NY)])]
  transfers between devices with their start and end apart: 10 -> 10, of which waited for: 3 -> 3; matrix products, arithmetic and copies ran while one was open for 1% -> 1% of each run, Pallas kernels for 6% -> 5%
where the time goes in v2:
time: 107 us; the launch traced here: 106 us
  starting transfers between devices  49.9 us (47%)
  blocking collectives  31.6 us (30%)
  waiting for transfers between devices  12.9 us (12%)
  Pallas kernels  8.41 us (8%)
  local copies, waits for them, and re-layouts  2.14 us (2%)
    all_to_all x1, blocking collectives, exchange(): return lax.all_to_all(array, axes, 0, 0, tiled=True)  31.6 us
    ppermute x4, starting transfers between devices, swap(): lax.ppermute(array, axis, [(i, i ^ bit) for i in range(dict(AXES)[axis])])  23.9 us
    all_to_all x3, starting transfers between devices, exchange(): return lax.all_to_all(array, axes, 0, 0, tiled=True)  19.4 us
    ppermute x3, waiting for transfers between devices, from_along_y(): return lax.ppermute(array, 'y', [((i + step) % NY, i) for i in range(NY)])  6.74 us
    ppermute x3, starting transfers between devices, from_along_y(): return lax.ppermute(array, 'y', [((i + step) % NY, i) for i in range(NY)])  6.53 us
    all_to_all x3, waiting for transfers between devices, exchange(): return lax.all_to_all(array, axes, 0, 0, tiled=True)  4.77 us
    pallas_call x1, Pallas kernels, gated_rows(): pl.pallas_call(gated_kernel, out_shape=jax.ShapeDtypeStruct((NC, NX, leng...  2.91 us
    pallas_call x1, Pallas kernels, run_states(): pl.pallas_call(run_states_kernel, out_shape=(jax.ShapeDtypeStruct((poles,...  2.77 us
  transfers between devices with their start and end apart: 10, of which 3 were waited for; matrix products, arithmetic and copies ran while one was open for 1% of the time, Pallas kernels for 5%

profile of v2, /device:TPU:1, one launch (start us, length us, event | category | flops | bytes accessed | tf_op | source)
XLA Modules:
  0.0 105.8 jit_solution(17438397789952004105)
XLA Ops:
  0.0 8.3 %collective-permute-start = (bf16[64,512]{1,0:T(8,128)(2,1)}, bf16[64,512]{1,0:T(8,128)(2,1)S(1)}, u32[]{:S(2)}, u32[]{:S(2)}) collective-permute-start(bf16[64,512]{1,0:T(8,128)(2,1)} %bitcast.18), channel_id=1, source_target_pairs={{0,32},{8,40},{16,48},{24,56},{32,0},{40,8},{48,16},{56,24},{1,33}... | collective-permute-start | bytes 196616 | tf_op jit(solution)/shard_map/ppermute | solution.py:168
  8.3 2.8 %run_states.1 = (f32[16,8,512]{2,1,0:T(8,128)}, bf16[8,16,512]{2,1,0:T(8,128)(2,1)}, f32[16,512]{1,0:T(8,128)}) custom-call(bf16[256,512]{1,0:T(8,128)(2,1)} %key_ref.3, bf16[256,512]{1,0:T(8,128)(2,1)} %value_ref.3, f32[16,512]{1,0:T(8,128)} %bitcast.16, f32[16,512]{1,0:T(8,128)} %bitcast.22), custom_call_target="tpu_custom_call" | custom-call | tf_op jit(solution)/shard_map/run_states/pallas_call | solution.py:47
  11.0 0.0 copy-start.2
  11.1 3.5 %all-to-all-start = ((bf16[8,16,512]{2,1,0:T(8,128)(2,1)}), bf16[8,16,512]{2,1,0:T(8,128)(2,1)S(1)}, u32[]{:S(2)}, u32[]{:S(2)}) async-start(bf16[8,16,512]{2,1,0:T(8,128)(2,1)} %get-tuple-element.12), calls=%async_computation | async-start | bytes 262144 | tf_op jit(solution)/shard_map/all_to_all | solution.py:180
  14.6 0.0 copy-start.6
  14.6 0.0 copy-done.2
  14.7 0.0 collective-permute-done
  14.7 0.7 copy-done.6
  15.4 10.6 %collective-permute-start.1 = (bf16[128,512]{1,0:T(8,128)(2,1)S(1)}, bf16[128,512]{1,0:T(8,128)(2,1)S(1)}, u32[]{:S(2)}, u32[]{:S(2)}) collective-permute-start(bf16[128,512]{1,0:T(8,128)(2,1)S(1)} %pad_maximum_fusion.2), channel_id=1, source_target_pairs={{0,64},{64,0},{1,65},{65,1},{2,66},{66,2},{3,67},{67,3},{4,68},{68... | collective-permute-start | bytes 393224 | tf_op jit(solution)/shard_map/ppermute | solution.py:168
  26.1 0.0 all-to-all-done
  26.1 0.2 fusion.1
  26.3 0.7 broadcast_in_dim.32
  26.9 0.0 copy-start.4
  26.9 8.8 %all-to-all-start.1 = ((bf16[8,16,512]{2,1,0:T(8,128)(2,1)}), bf16[8,16,512]{2,1,0:T(8,128)(2,1)S(1)}, u32[]{:S(2)}, u32[]{:S(2)}) async-start(bf16[8,16,512]{2,1,0:T(8,128)(2,1)} %broadcast_in_dim.32), calls=%async_computation.1 | async-start | bytes 262144 | tf_op jit(solution)/shard_map/all_to_all | solution.py:180
  35.7 0.0 collective-permute-done.1
  35.7 0.0 copy-start.1
  35.7 0.0 copy-start.3
  35.8 0.0 copy-start
  35.8 2.1 %collective-permute-start.3 = (bf16[256,512]{1,0:T(8,128)(2,1)S(1)}, bf16[256,512]{1,0:T(8,128)(2,1)S(1)}, u32[]{:S(2)}, u32[]{:S(2)}) collective-permute-start(bf16[256,512]{1,0:T(8,128)(2,1)S(1)} %pad_maximum_fusion.1), channel_id=1, source_target_pairs={{8,0},{16,8},{24,16},{32,24},{40,32},{48,40},{56,48},{0,56},{9,1},... | collective-permute-start | bytes 786440 | tf_op jit(solution)/shard_map/ppermute | solution.py:172
  37.8 2.6 %collective-permute-start.2 = (bf16[256,512]{1,0:T(8,128)(2,1)S(1)}, bf16[256,512]{1,0:T(8,128)(2,1)S(1)}, u32[]{:S(2)}, u32[]{:S(2)}) collective-permute-start(bf16[256,512]{1,0:T(8,128)(2,1)S(1)} %pad_maximum_fusion.1), channel_id=1, source_target_pairs={{16,0},{24,8},{32,16},{40,24},{48,32},{56,40},{0,48},{8,56},{17,1}... | collective-permute-start | bytes 786440 | tf_op jit(solution)/shard_map/ppermute | solution.py:172
  40.4 4.8 %all-to-all-done.1 = bf16[8,16,512]{2,1,0:T(8,128)(2,1)S(1)} async-done(((bf16[8,16,512]{2,1,0:T(8,128)(2,1)}), bf16[8,16,512]{2,1,0:T(8,128)(2,1)S(1)}, u32[]{:S(2)}, u32[]{:S(2)}) %all-to-all-start.1) | async-done | bytes 131104 | tf_op jit(solution)/shard_map/all_to_all | solution.py:180
  45.2 0.1 multiply_reduce_fusion
  45.3 0.0 copy-start.5
  45.3 0.0 copy-done.4
  45.4 0.0 copy-done.1
  45.4 0.0 copy-done.3
  45.4 0.0 copy-done
  45.4 0.7 copy-done.5
  46.1 2.9 %gated_rows.1 = bf16[2,4,128,512]{3,2,1,0:T(8,128)(2,1)} custom-call(bf16[256,512]{1,0:T(8,128)(2,1)S(1)} %copy-done.3, bf16[256,512]{1,0:T(8,128)(2,1)S(1)} %copy-done, bf16[256,512]{1,0:T(8,128)(2,1)S(1)} %copy-done.1, f32[16,512]{1,0:T(8,128)S(1)} %bitcast.17, f32[16,512]{1,0:T(8,128)S(1)} %copy-done.5, f32[16,8,512]{2,1,0:T(8,128)S(1)} %copy-done.4, ...), custom_call_target="tpu_custom_call" | custom-call | tf_op jit(solution)/shard_map/gated_rows/pallas_call | solution.py:106
  49.0 7.2 %all-to-all-start.2 = ((bf16[8,128,512]{2,1,0:T(8,128)(2,1)}), bf16[8,128,512]{2,1,0:T(8,128)(2,1)S(1)}, u32[]{:S(2)}, u32[]{:S(2)}) async-start(bf16[8,128,512]{2,1,0:T(8,128)(2,1)} %bitcast.6), calls=%async_computation.2 | async-start | bytes 2097152 | tf_op jit(solution)/shard_map/all_to_all | solution.py:180
  56.2 1.9 %collective-permute-start.4 = (bf16[256,512]{1,0:T(8,128)(2,1)S(1)}, bf16[256,512]{1,0:T(8,128)(2,1)S(1)}, u32[]{:S(2)}, u32[]{:S(2)}) collective-permute-start(bf16[256,512]{1,0:T(8,128)(2,1)S(1)} %pad_maximum_fusion.1), channel_id=1, source_target_pairs={{56,0},{0,8},{8,16},{16,24},{24,32},{32,40},{40,48},{48,56},{57,1}... | collective-permute-start | bytes 786440 | tf_op jit(solution)/shard_map/ppermute | solution.py:172
  58.1 0.0 collective-permute-done.2
  58.1 2.2 %collective-permute-start.5 = (bf16[512,512]{1,0:T(8,128)(2,1)S(1)}, bf16[512,512]{1,0:T(8,128)(2,1)S(1)}, u32[]{:S(2)}, u32[]{:S(2)}) collective-permute-start(bf16[512,512]{1,0:T(8,128)(2,1)S(1)} %pad_maximum_fusion.own_low), channel_id=1, source_target_pairs={{0,1},{1,0},{2,3},{3,2},{4,5},{5,4},{6,7},{7,6},{8,9},{9,8},{10,11... | collective-permute-start | bytes 1572872 | tf_op jit(solution)/shard_map/ppermute | solution.py:168
  60.3 0.0 collective-permute-done.3
  60.4 6.7 %collective-permute-done.4 = bf16[256,512]{1,0:T(8,128)(2,1)S(1)} collective-permute-done((bf16[256,512]{1,0:T(8,128)(2,1)S(1)}, bf16[256,512]{1,0:T(8,128)(2,1)S(1)}, u32[]{:S(2)}, u32[]{:S(2)}) %collective-permute-start.4) | collective-permute-done | bytes 262176 | tf_op jit(solution)/shard_map/ppermute | solution.py:172
  67.1 2.8 %collective-permute-start.6 = (bf16[512,512]{1,0:T(8,128)(2,1)S(1)}, bf16[512,512]{1,0:T(8,128)(2,1)S(1)}, u32[]{:S(2)}, u32[]{:S(2)}) collective-permute-start(bf16[512,512]{1,0:T(8,128)(2,1)S(1)} %constant_dynamic-update-slice_fusion.own_high), channel_id=1, source_target_pairs={{0,1},{1,0},{2,3},{3,2},{4,5},{5,4},{6,7},{7,6},{8,9},{9,8},{10,11... | collective-permute-start | bytes 1572872 | tf_op jit(solution)/shard_map/ppermute | solution.py:168
  69.9 0.1 pad_add_fusion.place_ref
  70.0 0.0 collective-permute-done.5.other_low
  70.0 1.4 %collective-permute-done.6.other_high = bf16[512,512]{1,0:T(8,128)(2,1)S(1)} collective-permute-done((bf16[512,512]{1,0:T(8,128)(2,1)S(1)}, bf16[512,512]{1,0:T(8,128)(2,1)S(1)}, u32[]{:S(2)}, u32[]{:S(2)}) %collective-permute-start.6) | collective-permute-done | bytes 524320 | tf_op jit(solution)/shard_map/ppermute | solution.py:168
  71.4 0.0 all-to-all-done.2
  71.4 1.9 %project.1 = bf16[4,4,32,1024]{3,2,1,0:T(8,128)(2,1)S(1)} custom-call(s32[3]{0:T(128)S(1)} %pad_add_fusion.place_ref, bf16[2,512,512]{2,1,0:T(8,128)(2,1)S(1)} %bitcast.13, bf16[512,512]{1,0:T(8,128)(2,1)S(1)} %pad_maximum_fusion.own_low, bf16[512,512]{1,0:T(8,128)(2,1)S(1)} %constant_dynamic-update-slice_fusion.own_high, ...), custom_call_target="tpu_custom_call" | custom-call | tf_op jit(solution)/shard_map/project/pallas_call | solution.py:138
  73.4 31.6 %all_to_all.20 = bf16[16,32,1024]{2,1,0:T(8,128)(2,1)S(1)} all-to-all(bf16[16,32,1024]{2,1,0:T(8,128)(2,1)S(1)} %bitcast.14), channel_id=1, replica_groups=mesh['x'=4,'h'=2,'y'=8,'z'=4,'c'=2] {'z','x'}, dimensions={0} | all-to-all | bytes 2097152 | tf_op jit(solution)/shard_map/all_to_all | solution.py:180
  105.0 0.8 finish.1
  (11 shorter events, 0.2 us)
Async XLA Ops:
  0.0 14.7 %collective-permute-start = (bf16[64,512]{1,0:T(8,128)(2,1)}, bf16[64,512]{1,0:T(8,128)(2,1)S(1)}, u32[]{:S(2)}, u32[]{:S(2)}) collective-permute-start(bf16[64,512]{1,0:T(8,128)(2,1)} %bitcast.18), channel_id=1, source_target_pairs={{0,32},{8,40},{16,48},{24,56},{32,0},{40,8},{48,16},{56,24},{1,33}... | collective-permute-start | bytes 196616 | tf_op jit(solution)/shard_map/ppermute | solution.py:168
  11.0 3.5 %copy-start.2 = (f32[512,16]{0,1:T(8,128)S(1)}, f32[512,16]{0,1:T(8,128)}, u32[]{:S(2)}) copy-start(f32[512,16]{0,1:T(8,128)} %param.9) | copy-start | bytes 98308
  11.1 15.0 %all-to-all-start = ((bf16[8,16,512]{2,1,0:T(8,128)(2,1)}), bf16[8,16,512]{2,1,0:T(8,128)(2,1)S(1)}, u32[]{:S(2)}, u32[]{:S(2)}) async-start(bf16[8,16,512]{2,1,0:T(8,128)(2,1)} %get-tuple-element.12), calls=%async_computation | async-start | bytes 262144 | tf_op jit(solution)/shard_map/all_to_all | solution.py:180
  14.6 0.8 copy-start.6
  15.4 20.3 %collective-permute-start.1 = (bf16[128,512]{1,0:T(8,128)(2,1)S(1)}, bf16[128,512]{1,0:T(8,128)(2,1)S(1)}, u32[]{:S(2)}, u32[]{:S(2)}) collective-permute-start(bf16[128,512]{1,0:T(8,128)(2,1)S(1)} %pad_maximum_fusion.2), channel_id=1, source_target_pairs={{0,64},{64,0},{1,65},{65,1},{2,66},{66,2},{3,67},{67,3},{4,68},{68... | collective-permute-start | bytes 393224 | tf_op jit(solution)/shard_map/ppermute | solution.py:168
  26.9 18.4 %copy-start.4 = (f32[16,8,512]{2,1,0:T(8,128)S(1)}, f32[16,8,512]{2,1,0:T(8,128)}, u32[]{:S(2)}) copy-start(f32[16,8,512]{2,1,0:T(8,128)} %get-tuple-element.11.runs_ref) | copy-start | bytes 786436
  26.9 18.2 %all-to-all-start.1 = ((bf16[8,16,512]{2,1,0:T(8,128)(2,1)}), bf16[8,16,512]{2,1,0:T(8,128)(2,1)S(1)}, u32[]{:S(2)}, u32[]{:S(2)}) async-start(bf16[8,16,512]{2,1,0:T(8,128)(2,1)} %broadcast_in_dim.32), calls=%async_computation.1 | async-start | bytes 262144 | tf_op jit(solution)/shard_map/all_to_all | solution.py:180
  35.7 9.6 %copy-start.1 = (bf16[256,512]{1,0:T(8,128)(2,1)S(1)}, bf16[256,512]{1,0:T(8,128)(2,1)}, u32[]{:S(2)}) copy-start(bf16[256,512]{1,0:T(8,128)(2,1)} %value_ref.3) | copy-start | bytes 786436
  35.7 9.6 %copy-start.3 = (bf16[256,512]{1,0:T(8,128)(2,1)S(1)}, bf16[256,512]{1,0:T(8,128)(2,1)}, u32[]{:S(2)}) copy-start(bf16[256,512]{1,0:T(8,128)(2,1)} %gate_ref.1) | copy-start | bytes 786436
  35.8 9.6 %copy-start = (bf16[256,512]{1,0:T(8,128)(2,1)S(1)}, bf16[256,512]{1,0:T(8,128)(2,1)}, u32[]{:S(2)}) copy-start(bf16[256,512]{1,0:T(8,128)(2,1)} %key_ref.3) | copy-start | bytes 786436
  35.8 24.6 %collective-permute-start.3 = (bf16[256,512]{1,0:T(8,128)(2,1)S(1)}, bf16[256,512]{1,0:T(8,128)(2,1)S(1)}, u32[]{:S(2)}, u32[]{:S(2)}) collective-permute-start(bf16[256,512]{1,0:T(8,128)(2,1)S(1)} %pad_maximum_fusion.1), channel_id=1, source_target_pairs={{8,0},{16,8},{24,16},{32,24},{40,32},{48,40},{56,48},{0,56},{9,1},... | collective-permute-start | bytes 786440 | tf_op jit(solution)/shard_map/ppermute | solution.py:172
  37.8 20.2 %collective-permute-start.2 = (bf16[256,512]{1,0:T(8,128)(2,1)S(1)}, bf16[256,512]{1,0:T(8,128)(2,1)S(1)}, u32[]{:S(2)}, u32[]{:S(2)}) collective-permute-start(bf16[256,512]{1,0:T(8,128)(2,1)S(1)} %pad_maximum_fusion.1), channel_id=1, source_target_pairs={{16,0},{24,8},{32,16},{40,24},{48,32},{56,40},{0,48},{8,56},{17,1}... | collective-permute-start | bytes 786440 | tf_op jit(solution)/shard_map/ppermute | solution.py:172
  45.3 0.8 copy-start.5
  49.0 22.5 %all-to-all-start.2 = ((bf16[8,128,512]{2,1,0:T(8,128)(2,1)}), bf16[8,128,512]{2,1,0:T(8,128)(2,1)S(1)}, u32[]{:S(2)}, u32[]{:S(2)}) async-start(bf16[8,128,512]{2,1,0:T(8,128)(2,1)} %bitcast.6), calls=%async_computation.2 | async-start | bytes 2097152 | tf_op jit(solution)/shard_map/all_to_all | solution.py:180
  56.2 11.0 %collective-permute-start.4 = (bf16[256,512]{1,0:T(8,128)(2,1)S(1)}, bf16[256,512]{1,0:T(8,128)(2,1)S(1)}, u32[]{:S(2)}, u32[]{:S(2)}) collective-permute-start(bf16[256,512]{1,0:T(8,128)(2,1)S(1)} %pad_maximum_fusion.1), channel_id=1, source_target_pairs={{56,0},{0,8},{8,16},{16,24},{24,32},{32,40},{40,48},{48,56},{57,1}... | collective-permute-start | bytes 786440 | tf_op jit(solution)/shard_map/ppermute | solution.py:172
  58.1 11.9 %collective-permute-start.5 = (bf16[512,512]{1,0:T(8,128)(2,1)S(1)}, bf16[512,512]{1,0:T(8,128)(2,1)S(1)}, u32[]{:S(2)}, u32[]{:S(2)}) collective-permute-start(bf16[512,512]{1,0:T(8,128)(2,1)S(1)} %pad_maximum_fusion.own_low), channel_id=1, source_target_pairs={{0,1},{1,0},{2,3},{3,2},{4,5},{5,4},{6,7},{7,6},{8,9},{9,8},{10,11... | collective-permute-start | bytes 1572872 | tf_op jit(solution)/shard_map/ppermute | solution.py:168
  67.1 4.3 %collective-permute-start.6 = (bf16[512,512]{1,0:T(8,128)(2,1)S(1)}, bf16[512,512]{1,0:T(8,128)(2,1)S(1)}, u32[]{:S(2)}, u32[]{:S(2)}) collective-permute-start(bf16[512,512]{1,0:T(8,128)(2,1)S(1)} %constant_dynamic-update-slice_fusion.own_high), channel_id=1, source_target_pairs={{0,1},{1,0},{2,3},{3,2},{4,5},{5,4},{6,7},{7,6},{8,9},{9,8},{10,11... | collective-permute-start | bytes 1572872 | tf_op jit(solution)/shard_map/ppermute | solution.py:168

commit v3 on v2

--- a/solution.py
+++ b/solution.py
@@ -17,9 +17,11 @@
 bf16 = jnp.bfloat16
 
 
-def run_states_kernel(key_ref, value_ref, rate_ref, residue_ref, runs_ref, block_ref, weight_ref, signal):
-    weight_ref[...] = residue_ref[...] * jnp.sqrt(rate_ref[...])
+def run_states_kernel(key_ref, value_ref, rate_ref, residue_ref, runs_ref, block_ref, signal):
     poles, chans = rate_ref.shape
+    for r in range(0, poles, SUB):
+        at = pl.ds(r, SUB)
+        runs_ref[poles + r // SUB] = residue_ref[at, :] * jnp.sqrt(rate_ref[at, :])
     steps = key_ref.shape[0] // SUB
     later = (SUB - 1 - lax.broadcasted_iota(jnp.int32, (SUB, LANES), 0)).astype(f32) * steps
     for tile in range(chans // LANES):
@@ -47,9 +49,8 @@
     return pl.pallas_call(
         run_states_kernel,
         out_shape=(
-            jax.ShapeDtypeStruct((poles, SUB, chans), f32),
+            jax.ShapeDtypeStruct((poles + poles // SUB, SUB, chans), f32),
             jax.ShapeDtypeStruct((NY, poles, chans), bf16),
-            jax.ShapeDtypeStruct((poles, chans), f32),
         ),
         scratch_shapes=[pltpu.VMEM((key_input.shape[0], LANES), f32)],
         compiler_params=pltpu.CompilerParams(vmem_limit_bytes=60 << 20),
@@ -57,7 +58,7 @@
     )(key_input, value_input, rate, residue)
 
 
-def gated_kernel(gate_ref, key_ref, value_ref, rate_ref, weight_ref, runs_ref, before_ref, out_ref, signal, conv):
+def gated_kernel(gate_ref, key_ref, value_ref, rate_ref, runs_ref, before_ref, out_ref, signal, conv):
     poles, chans = rate_ref.shape
     steps = key_ref.shape[0] // SUB
     for tile in range(chans // LANES):
@@ -78,7 +79,8 @@
             start = jnp.where(run >= 1, pltpu.roll(ends, 1, 0), 0.0)
             starts.append(start + jnp.exp(-rate * (steps * run_f)) * before)
             decays.append(jnp.exp(-rate))
-            weights.append(jnp.broadcast_to(weight_ref[pl.ds(r, 1), lanes], (SUB, LANES)))
+            weight = runs_ref[poles + r // SUB, pl.ds(r % SUB, 1), lanes]
+            weights.append(jnp.broadcast_to(weight, (SUB, LANES)))
 
         def step(j, states):
             at = pl.ds(j, SUB, stride=steps)
@@ -101,7 +103,7 @@
                 out_ref[part % NC, copy, pl.ds(part // NC * rows, rows), lanes] = piece
 
 
-def gated_rows(gate_input, key_input, value_input, rate, pole_weight, runs, before):
+def gated_rows(gate_input, key_input, value_input, rate, runs, before):
     length, chans = gate_input.shape
     return pl.pallas_call(
         gated_kernel,
@@ -109,7 +111,7 @@
         scratch_shapes=[pltpu.VMEM((chans // LANES, length, LANES), f32)] * 2,
         compiler_params=pltpu.CompilerParams(vmem_limit_bytes=32 << 20),
         name="gated_rows",
-    )(gate_input, key_input, value_input, rate, pole_weight, runs, before)
+    )(gate_input, key_input, value_input, rate, runs, before)
 
 
 def project_kernel(place_ref, rows_ref, own_low, own_high, other_low, other_high, out_ref, own, other):
@@ -118,7 +120,7 @@
     half = blocks // 2
     width = own_low.shape[0] // half
     for p in range(blocks):
-        step, b, a = (0, *RING)[p // 4], p // 2 % 2, p % 2
+        step, a, b = (0, *RING)[p // 4], p // 2 % 2, p % 2
         block = (h + b) % NH * NY + (y + step + 4 * a + NY) % NY
         at = pl.ds(pl.multiple_of(block * width, width), width)
         of = pl.ds(p % half * width, width)
@@ -190,11 +192,11 @@
     rate, residue = decay_rate.T, residues.T
 
     weight = out_weight.T
+    other = swap(weight, "h", 1)
+
+    runs, block = run_states(key_input, value_input, rate, residue)
+    weight = with_other(weight, other)
     other = swap(weight, "y", 4)
-
-    runs, block, pole_weight = run_states(key_input, value_input, rate, residue)
-    weight = with_other(weight, other)
-    other = swap(weight, "h", 1)
 
     blocks = exchange(block, "y")
     blocks = blocks.astype(f32)
@@ -214,7 +216,7 @@
     )
     before = inner + jnp.exp(-rate * (length * y).astype(f32)) * outer
 
-    rows = gated_rows(gate_input, key_input, value_input, rate, pole_weight, runs, before)
+    rows = gated_rows(gate_input, key_input, value_input, rate, runs, before)
     late, rows = lax.optimization_barrier((weight, rows))
     others.append(from_along_y(late, RING[2]))
     arrived = exchange(rows.reshape(NC * NX, length // NC, chans), ("c", "x")).reshape(NC, -1, chans)

time: 107 us -> 105 us (0.981)
  waiting for transfers between devices: 12.9 us -> 9 us
  starting transfers between devices: 49.9 us -> 52.7 us
    ppermute x3, starting transfers between devices: 6.53 us -> 9.28 us  [from_along_y(): return lax.ppermute(array, 'y', [((i + step) % NY, i) for i in range(NY)])]
    all_to_all x3, waiting for transfers between devices: 4.77 us -> 2.11 us  [exchange(): return lax.all_to_all(array, axes, 0, 0, tiled=True)]
    ppermute x3, waiting for transfers between devices: 6.74 us -> 5.46 us  [from_along_y(): return lax.ppermute(array, 'y', [((i + step) % NY, i) for i in range(NY)])]
where the time goes in v3:
time: 105 us; the launch traced here: 104 us
  starting transfers between devices  52.7 us (50%)
  blocking collectives  31.6 us (30%)
  waiting for transfers between devices  9 us (9%)
  Pallas kernels  8.42 us (8%)
  local copies, waits for them, and re-layouts  1.46 us (1%)
    all_to_all x1, blocking collectives, exchange(): return lax.all_to_all(array, axes, 0, 0, tiled=True)  31.6 us
    ppermute x4, starting transfers between devices, swap(): lax.ppermute(array, axis, [(i, i ^ bit) for i in range(dict(AXES)[axis])])  24.9 us
    all_to_all x3, starting transfers between devices, exchange(): return lax.all_to_all(array, axes, 0, 0, tiled=True)  18.5 us
    ppermute x3, starting transfers between devices, from_along_y(): return lax.ppermute(array, 'y', [((i + step) % NY, i) for i in range(NY)])  9.28 us
    ppermute x3, waiting for transfers between devices, from_along_y(): return lax.ppermute(array, 'y', [((i + step) % NY, i) for i in range(NY)])  5.46 us
    pallas_call x1, Pallas kernels, gated_rows(): pl.pallas_call(gated_kernel, out_shape=jax.ShapeDtypeStruct((NC, NX, leng...  2.9 us
    pallas_call x1, Pallas kernels, run_states(): pl.pallas_call(run_states_kernel, out_shape=(jax.ShapeDtypeStruct((poles...  2.78 us
    all_to_all x3, waiting for transfers between devices, exchange(): return lax.all_to_all(array, axes, 0, 0, tiled=True)  2.11 us
  transfers between devices with their start and end apart: 10, of which 3 were waited for; matrix products, arithmetic and copies ran while one was open for 1% of the time, Pallas kernels for 5%

profile of v3, /device:TPU:1, one launch (start us, length us, event | category | flops | bytes accessed | tf_op | source)
XLA Modules:
  0.0 104.0 jit_solution(1075903544894340033)
XLA Ops:
  0.0 11.5 %collective-permute-start = (bf16[64,512]{1,0:T(8,128)(2,1)}, bf16[64,512]{1,0:T(8,128)(2,1)S(1)}, u32[]{:S(2)}, u32[]{:S(2)}) collective-permute-start(bf16[64,512]{1,0:T(8,128)(2,1)} %bitcast.18), channel_id=1, source_target_pairs={{0,64},{64,0},{1,65},{65,1},{2,66},{66,2},{3,67},{67,3},{4,68},{68... | collective-permute-start | bytes 196616 | tf_op jit(solution)/shard_map/ppermute | solution.py:170
  11.5 2.8 %run_states.1 = (f32[18,8,512]{2,1,0:T(8,128)}, bf16[8,16,512]{2,1,0:T(8,128)(2,1)}) custom-call(bf16[256,512]{1,0:T(8,128)(2,1)} %key_ref.3, bf16[256,512]{1,0:T(8,128)(2,1)} %value_ref.3, f32[16,512]{1,0:T(8,128)} %bitcast.16, f32[16,512]{1,0:T(8,128)} %bitcast.22), custom_call_target="tpu_custom_call" | custom-call | tf_op jit(solution)/shard_map/run_states/pallas_call | solution.py:49
  14.2 0.0 copy-start.2
  14.2 7.0 %all-to-all-start = ((bf16[8,16,512]{2,1,0:T(8,128)(2,1)}), bf16[8,16,512]{2,1,0:T(8,128)(2,1)S(1)}, u32[]{:S(2)}, u32[]{:S(2)}) async-start(bf16[8,16,512]{2,1,0:T(8,128)(2,1)} %get-tuple-element.10), calls=%async_computation | async-start | bytes 262144 | tf_op jit(solution)/shard_map/all_to_all | solution.py:182
  21.2 0.0 copy-start.5
  21.2 0.0 copy-done.2
  21.3 0.0 collective-permute-done
  21.3 0.7 copy-done.5
  22.1 7.3 %collective-permute-start.1 = (bf16[128,512]{1,0:T(8,128)(2,1)S(1)}, bf16[128,512]{1,0:T(8,128)(2,1)S(1)}, u32[]{:S(2)}, u32[]{:S(2)}) collective-permute-start(bf16[128,512]{1,0:T(8,128)(2,1)S(1)} %pad_maximum_fusion.2), channel_id=1, source_target_pairs={{0,32},{8,40},{16,48},{24,56},{32,0},{40,8},{48,16},{56,24},{1,33}... | collective-permute-start | bytes 393224 | tf_op jit(solution)/shard_map/ppermute | solution.py:170
  29.3 0.0 all-to-all-done
  29.4 0.2 fusion.1
  29.6 0.7 broadcast_in_dim.32
  30.2 0.0 copy-start.4
  30.2 4.2 %all-to-all-start.1 = ((bf16[8,16,512]{2,1,0:T(8,128)(2,1)}), bf16[8,16,512]{2,1,0:T(8,128)(2,1)S(1)}, u32[]{:S(2)}, u32[]{:S(2)}) async-start(bf16[8,16,512]{2,1,0:T(8,128)(2,1)} %broadcast_in_dim.32), calls=%async_computation.1 | async-start | bytes 262144 | tf_op jit(solution)/shard_map/all_to_all | solution.py:182
  34.4 0.0 collective-permute-done.1
  34.4 0.0 copy-start.1
  34.4 0.0 copy-start.3
  34.4 0.0 copy-start
  34.5 4.4 %collective-permute-start.3 = (bf16[256,512]{1,0:T(8,128)(2,1)S(1)}, bf16[256,512]{1,0:T(8,128)(2,1)S(1)}, u32[]{:S(2)}, u32[]{:S(2)}) collective-permute-start(bf16[256,512]{1,0:T(8,128)(2,1)S(1)} %pad_maximum_fusion.1), channel_id=1, source_target_pairs={{8,0},{16,8},{24,16},{32,24},{40,32},{48,40},{56,48},{0,56},{9,1},... | collective-permute-start | bytes 786440 | tf_op jit(solution)/shard_map/ppermute | solution.py:174
  38.9 2.9 %collective-permute-start.2 = (bf16[256,512]{1,0:T(8,128)(2,1)S(1)}, bf16[256,512]{1,0:T(8,128)(2,1)S(1)}, u32[]{:S(2)}, u32[]{:S(2)}) collective-permute-start(bf16[256,512]{1,0:T(8,128)(2,1)S(1)} %pad_maximum_fusion.1), channel_id=1, source_target_pairs={{16,0},{24,8},{32,16},{40,24},{48,32},{56,40},{0,48},{8,56},{17,1}... | collective-permute-start | bytes 786440 | tf_op jit(solution)/shard_map/ppermute | solution.py:174
  41.8 2.1 %all-to-all-done.1 = bf16[8,16,512]{2,1,0:T(8,128)(2,1)S(1)} async-done(((bf16[8,16,512]{2,1,0:T(8,128)(2,1)}), bf16[8,16,512]{2,1,0:T(8,128)(2,1)S(1)}, u32[]{:S(2)}, u32[]{:S(2)}) %all-to-all-start.1) | async-done | bytes 131104 | tf_op jit(solution)/shard_map/all_to_all | solution.py:182
  43.9 0.1 multiply_reduce_fusion
  44.0 0.0 copy-done.4
  44.0 0.0 copy-done.1
  44.0 0.0 copy-done.3
  44.0 0.0 copy-done
  44.1 2.9 %gated_rows.1 = bf16[2,4,128,512]{3,2,1,0:T(8,128)(2,1)} custom-call(bf16[256,512]{1,0:T(8,128)(2,1)S(1)} %copy-done.4, bf16[256,512]{1,0:T(8,128)(2,1)S(1)} %copy-done, bf16[256,512]{1,0:T(8,128)(2,1)S(1)} %copy-done.1, f32[16,512]{1,0:T(8,128)S(1)} %bitcast.17, f32[18,8,512]{2,1,0:T(8,128)S(1)} %copy-done.3, f32[16,512]{1,0:T(8,128)S(1)} %multiply_add_fusion.before_ref), custom_call_target="tpu_custom_call" | custom-call | tf_op jit(solution)/shard_map/gated_rows/pallas_call | solution.py:108
  47.0 7.4 %all-to-all-start.2 = ((bf16[8,128,512]{2,1,0:T(8,128)(2,1)}), bf16[8,128,512]{2,1,0:T(8,128)(2,1)S(1)}, u32[]{:S(2)}, u32[]{:S(2)}) async-start(bf16[8,128,512]{2,1,0:T(8,128)(2,1)} %bitcast.6), calls=%async_computation.2 | async-start | bytes 2097152 | tf_op jit(solution)/shard_map/all_to_all | solution.py:182
  54.3 2.0 %collective-permute-start.4 = (bf16[256,512]{1,0:T(8,128)(2,1)S(1)}, bf16[256,512]{1,0:T(8,128)(2,1)S(1)}, u32[]{:S(2)}, u32[]{:S(2)}) collective-permute-start(bf16[256,512]{1,0:T(8,128)(2,1)S(1)} %pad_maximum_fusion.1), channel_id=1, source_target_pairs={{56,0},{0,8},{8,16},{16,24},{24,32},{32,40},{40,48},{48,56},{57,1}... | collective-permute-start | bytes 786440 | tf_op jit(solution)/shard_map/ppermute | solution.py:174
  56.3 0.0 collective-permute-done.2
  56.4 3.4 %collective-permute-start.5 = (bf16[512,512]{1,0:T(8,128)(2,1)S(1)}, bf16[512,512]{1,0:T(8,128)(2,1)S(1)}, u32[]{:S(2)}, u32[]{:S(2)}) collective-permute-start(bf16[512,512]{1,0:T(8,128)(2,1)S(1)} %pad_maximum_fusion.own_low), channel_id=1, source_target_pairs={{0,1},{1,0},{2,3},{3,2},{4,5},{5,4},{6,7},{7,6},{8,9},{9,8},{10,11... | collective-permute-start | bytes 1572872 | tf_op jit(solution)/shard_map/ppermute | solution.py:170
  59.8 0.0 collective-permute-done.3
  59.8 5.5 %collective-permute-done.4 = bf16[256,512]{1,0:T(8,128)(2,1)S(1)} collective-permute-done((bf16[256,512]{1,0:T(8,128)(2,1)S(1)}, bf16[256,512]{1,0:T(8,128)(2,1)S(1)}, u32[]{:S(2)}, u32[]{:S(2)}) %collective-permute-start.4) | collective-permute-done | bytes 262176 | tf_op jit(solution)/shard_map/ppermute | solution.py:174
  65.3 2.8 %collective-permute-start.6 = (bf16[512,512]{1,0:T(8,128)(2,1)S(1)}, bf16[512,512]{1,0:T(8,128)(2,1)S(1)}, u32[]{:S(2)}, u32[]{:S(2)}) collective-permute-start(bf16[512,512]{1,0:T(8,128)(2,1)S(1)} %constant_dynamic-update-slice_fusion.own_high), channel_id=1, source_target_pairs={{0,1},{1,0},{2,3},{3,2},{4,5},{5,4},{6,7},{7,6},{8,9},{9,8},{10,11... | collective-permute-start | bytes 1572872 | tf_op jit(solution)/shard_map/ppermute | solution.py:170
  68.1 0.1 pad_add_fusion.place_ref
  68.2 0.0 collective-permute-done.5.other_low
  68.2 1.4 %collective-permute-done.6.other_high = bf16[512,512]{1,0:T(8,128)(2,1)S(1)} collective-permute-done((bf16[512,512]{1,0:T(8,128)(2,1)S(1)}, bf16[512,512]{1,0:T(8,128)(2,1)S(1)}, u32[]{:S(2)}, u32[]{:S(2)}) %collective-permute-start.6) | collective-permute-done | bytes 524320 | tf_op jit(solution)/shard_map/ppermute | solution.py:170
  69.6 0.0 all-to-all-done.2
  69.6 1.9 %project.1 = bf16[4,4,32,1024]{3,2,1,0:T(8,128)(2,1)S(1)} custom-call(s32[3]{0:T(128)S(1)} %pad_add_fusion.place_ref, bf16[2,512,512]{2,1,0:T(8,128)(2,1)S(1)} %bitcast.13, bf16[512,512]{1,0:T(8,128)(2,1)S(1)} %pad_maximum_fusion.own_low, bf16[512,512]{1,0:T(8,128)(2,1)S(1)} %constant_dynamic-update-slice_fusion.own_high, ...), custom_call_target="tpu_custom_call" | custom-call | tf_op jit(solution)/shard_map/project/pallas_call | solution.py:140
  71.5 31.6 %all_to_all.20 = bf16[16,32,1024]{2,1,0:T(8,128)(2,1)S(1)} all-to-all(bf16[16,32,1024]{2,1,0:T(8,128)(2,1)S(1)} %bitcast.14), channel_id=1, replica_groups=mesh['x'=4,'h'=2,'y'=8,'z'=4,'c'=2] {'z','x'}, dimensions={0} | all-to-all | bytes 2097152 | tf_op jit(solution)/shard_map/all_to_all | solution.py:182
  103.2 0.8 finish.1
  (11 shorter events, 0.2 us)
Async XLA Ops:
  0.0 21.3 %collective-permute-start = (bf16[64,512]{1,0:T(8,128)(2,1)}, bf16[64,512]{1,0:T(8,128)(2,1)S(1)}, u32[]{:S(2)}, u32[]{:S(2)}) collective-permute-start(bf16[64,512]{1,0:T(8,128)(2,1)} %bitcast.18), channel_id=1, source_target_pairs={{0,64},{64,0},{1,65},{65,1},{2,66},{66,2},{3,67},{67,3},{4,68},{68... | collective-permute-start | bytes 196616 | tf_op jit(solution)/shard_map/ppermute | solution.py:170
  14.2 7.0 %copy-start.2 = (f32[512,16]{0,1:T(8,128)S(1)}, f32[512,16]{0,1:T(8,128)}, u32[]{:S(2)}) copy-start(f32[512,16]{0,1:T(8,128)} %param.9) | copy-start | bytes 98308
  14.2 15.1 %all-to-all-start = ((bf16[8,16,512]{2,1,0:T(8,128)(2,1)}), bf16[8,16,512]{2,1,0:T(8,128)(2,1)S(1)}, u32[]{:S(2)}, u32[]{:S(2)}) async-start(bf16[8,16,512]{2,1,0:T(8,128)(2,1)} %get-tuple-element.10), calls=%async_computation | async-start | bytes 262144 | tf_op jit(solution)/shard_map/all_to_all | solution.py:182
  21.2 0.8 copy-start.5
  22.1 12.3 %collective-permute-start.1 = (bf16[128,512]{1,0:T(8,128)(2,1)S(1)}, bf16[128,512]{1,0:T(8,128)(2,1)S(1)}, u32[]{:S(2)}, u32[]{:S(2)}) collective-permute-start(bf16[128,512]{1,0:T(8,128)(2,1)S(1)} %pad_maximum_fusion.2), channel_id=1, source_target_pairs={{0,32},{8,40},{16,48},{24,56},{32,0},{40,8},{48,16},{56,24},{1,33}... | collective-permute-start | bytes 393224 | tf_op jit(solution)/shard_map/ppermute | solution.py:170
  30.2 13.8 %copy-start.4 = (bf16[256,512]{1,0:T(8,128)(2,1)S(1)}, bf16[256,512]{1,0:T(8,128)(2,1)}, u32[]{:S(2)}) copy-start(bf16[256,512]{1,0:T(8,128)(2,1)} %gate_ref.1) | copy-start | bytes 786436
  30.2 13.6 %all-to-all-start.1 = ((bf16[8,16,512]{2,1,0:T(8,128)(2,1)}), bf16[8,16,512]{2,1,0:T(8,128)(2,1)S(1)}, u32[]{:S(2)}, u32[]{:S(2)}) async-start(bf16[8,16,512]{2,1,0:T(8,128)(2,1)} %broadcast_in_dim.32), calls=%async_computation.1 | async-start | bytes 262144 | tf_op jit(solution)/shard_map/all_to_all | solution.py:182
  34.4 9.6 %copy-start.1 = (bf16[256,512]{1,0:T(8,128)(2,1)S(1)}, bf16[256,512]{1,0:T(8,128)(2,1)}, u32[]{:S(2)}) copy-start(bf16[256,512]{1,0:T(8,128)(2,1)} %value_ref.3) | copy-start | bytes 786436
  34.4 9.6 %copy-start.3 = (f32[18,8,512]{2,1,0:T(8,128)S(1)}, f32[18,8,512]{2,1,0:T(8,128)}, u32[]{:S(2)}) copy-start(f32[18,8,512]{2,1,0:T(8,128)} %get-tuple-element.9.runs_ref) | copy-start | bytes 884740
  34.4 9.6 %copy-start = (bf16[256,512]{1,0:T(8,128)(2,1)S(1)}, bf16[256,512]{1,0:T(8,128)(2,1)}, u32[]{:S(2)}) copy-start(bf16[256,512]{1,0:T(8,128)(2,1)} %key_ref.3) | copy-start | bytes 786436
  34.5 25.3 %collective-permute-start.3 = (bf16[256,512]{1,0:T(8,128)(2,1)S(1)}, bf16[256,512]{1,0:T(8,128)(2,1)S(1)}, u32[]{:S(2)}, u32[]{:S(2)}) collective-permute-start(bf16[256,512]{1,0:T(8,128)(2,1)S(1)} %pad_maximum_fusion.1), channel_id=1, source_target_pairs={{8,0},{16,8},{24,16},{32,24},{40,32},{48,40},{56,48},{0,56},{9,1},... | collective-permute-start | bytes 786440 | tf_op jit(solution)/shard_map/ppermute | solution.py:174
  38.9 17.5 %collective-permute-start.2 = (bf16[256,512]{1,0:T(8,128)(2,1)S(1)}, bf16[256,512]{1,0:T(8,128)(2,1)S(1)}, u32[]{:S(2)}, u32[]{:S(2)}) collective-permute-start(bf16[256,512]{1,0:T(8,128)(2,1)S(1)} %pad_maximum_fusion.1), channel_id=1, source_target_pairs={{16,0},{24,8},{32,16},{40,24},{48,32},{56,40},{0,48},{8,56},{17,1}... | collective-permute-start | bytes 786440 | tf_op jit(solution)/shard_map/ppermute | solution.py:174
  47.0 22.7 %all-to-all-start.2 = ((bf16[8,128,512]{2,1,0:T(8,128)(2,1)}), bf16[8,128,512]{2,1,0:T(8,128)(2,1)S(1)}, u32[]{:S(2)}, u32[]{:S(2)}) async-start(bf16[8,128,512]{2,1,0:T(8,128)(2,1)} %bitcast.6), calls=%async_computation.2 | async-start | bytes 2097152 | tf_op jit(solution)/shard_map/all_to_all | solution.py:182
  54.3 11.0 %collective-permute-start.4 = (bf16[256,512]{1,0:T(8,128)(2,1)S(1)}, bf16[256,512]{1,0:T(8,128)(2,1)S(1)}, u32[]{:S(2)}, u32[]{:S(2)}) collective-permute-start(bf16[256,512]{1,0:T(8,128)(2,1)S(1)} %pad_maximum_fusion.1), channel_id=1, source_target_pairs={{56,0},{0,8},{8,16},{16,24},{24,32},{32,40},{40,48},{48,56},{57,1}... | collective-permute-start | bytes 786440 | tf_op jit(solution)/shard_map/ppermute | solution.py:174
  56.4 11.8 %collective-permute-start.5 = (bf16[512,512]{1,0:T(8,128)(2,1)S(1)}, bf16[512,512]{1,0:T(8,128)(2,1)S(1)}, u32[]{:S(2)}, u32[]{:S(2)}) collective-permute-start(bf16[512,512]{1,0:T(8,128)(2,1)S(1)} %pad_maximum_fusion.own_low), channel_id=1, source_target_pairs={{0,1},{1,0},{2,3},{3,2},{4,5},{5,4},{6,7},{7,6},{8,9},{9,8},{10,11... | collective-permute-start | bytes 1572872 | tf_op jit(solution)/shard_map/ppermute | solution.py:170
  65.3 4.3 %collective-permute-start.6 = (bf16[512,512]{1,0:T(8,128)(2,1)S(1)}, bf16[512,512]{1,0:T(8,128)(2,1)S(1)}, u32[]{:S(2)}, u32[]{:S(2)}) collective-permute-start(bf16[512,512]{1,0:T(8,128)(2,1)S(1)} %constant_dynamic-update-slice_fusion.own_high), channel_id=1, source_target_pairs={{0,1},{1,0},{2,3},{3,2},{4,5},{5,4},{6,7},{7,6},{8,9},{9,8},{10,11... | collective-permute-start | bytes 1572872 | tf_op jit(solution)/shard_map/ppermute | solution.py:170

commit v4 on v3

--- a/solution.py
+++ b/solution.py
@@ -9,7 +9,7 @@
 NX, NH, NY, NZ, NC = (size for _, size in AXES)
 SEQ = ("x", "h", "y")
 CH = ("z", "c")
-RING = (2, 1, -1)
+RING = (2, -1, 1)
 
 SUB = 8
 LANES = 128

time: 105 us -> 104 us (level)
  starting transfers between devices: 52.7 us -> 51.4 us
    ppermute x4, starting transfers between devices: 24.9 us -> 23.5 us  [swap(): lax.ppermute(array, axis, [(i, i ^ bit) for i in range(dict(AXES)[axis])])]
  transfers between devices with their start and end apart: 10 -> 10, of which waited for: 3 -> 4; matrix products, arithmetic and copies ran while one was open for 1% -> 1% of each run, Pallas kernels for 5% -> 6%
where the time goes in v4:
time: 104 us; the launch traced here: 103 us
  starting transfers between devices  51.4 us (49%)
  blocking collectives  30.7 us (30%)
  waiting for transfers between devices  9.96 us (10%)
  Pallas kernels  8.42 us (8%)
  local copies, waits for them, and re-layouts  1.46 us (1%)
    all_to_all x1, blocking collectives, exchange(): return lax.all_to_all(array, axes, 0, 0, tiled=True)  30.7 us
    ppermute x4, starting transfers between devices, swap(): lax.ppermute(array, axis, [(i, i ^ bit) for i in range(dict(AXES)[axis])])  23.5 us
    all_to_all x3, starting transfers between devices, exchange(): return lax.all_to_all(array, axes, 0, 0, tiled=True)  18.5 us
    ppermute x3, starting transfers between devices, from_along_y(): return lax.ppermute(array, 'y', [((i + step) % NY, i) for i in range(NY)])  9.42 us
    ppermute x3, waiting for transfers between devices, from_along_y(): return lax.ppermute(array, 'y', [((i + step) % NY, i) for i in range(NY)])  5.73 us
    pallas_call x1, Pallas kernels, gated_rows(): pl.pallas_call(gated_kernel, out_shape=jax.ShapeDtypeStruct((NC, NX, leng...  2.9 us
    all_to_all x3, waiting for transfers between devices, exchange(): return lax.all_to_all(array, axes, 0, 0, tiled=True)  2.79 us
    pallas_call x1, Pallas kernels, run_states(): pl.pallas_call(run_states_kernel, out_shape=(jax.ShapeDtypeStruct((poles...  2.78 us
  transfers between devices with their start and end apart: 10, of which 4 were waited for; matrix products, arithmetic and copies ran while one was open for 1% of the time, Pallas kernels for 6%

profile of v4, /device:TPU:1, one launch (start us, length us, event | category | flops | bytes accessed | tf_op | source)
XLA Modules:
  0.0 102.8 jit_solution(2751563857333720414)
XLA Ops:
  0.0 11.5 %collective-permute-start = (bf16[64,512]{1,0:T(8,128)(2,1)}, bf16[64,512]{1,0:T(8,128)(2,1)S(1)}, u32[]{:S(2)}, u32[]{:S(2)}) collective-permute-start(bf16[64,512]{1,0:T(8,128)(2,1)} %bitcast.18), channel_id=1, source_target_pairs={{0,64},{64,0},{1,65},{65,1},{2,66},{66,2},{3,67},{67,3},{4,68},{68... | collective-permute-start | bytes 196616 | tf_op jit(solution)/shard_map/ppermute | solution.py:170
  11.5 2.8 %run_states.1 = (f32[18,8,512]{2,1,0:T(8,128)}, bf16[8,16,512]{2,1,0:T(8,128)(2,1)}) custom-call(bf16[256,512]{1,0:T(8,128)(2,1)} %key_ref.3, bf16[256,512]{1,0:T(8,128)(2,1)} %value_ref.3, f32[16,512]{1,0:T(8,128)} %bitcast.16, f32[16,512]{1,0:T(8,128)} %bitcast.22), custom_call_target="tpu_custom_call" | custom-call | tf_op jit(solution)/shard_map/run_states/pallas_call | solution.py:49
  14.2 0.0 copy-start.2
  14.2 7.0 %all-to-all-start = ((bf16[8,16,512]{2,1,0:T(8,128)(2,1)}), bf16[8,16,512]{2,1,0:T(8,128)(2,1)S(1)}, u32[]{:S(2)}, u32[]{:S(2)}) async-start(bf16[8,16,512]{2,1,0:T(8,128)(2,1)} %get-tuple-element.10), calls=%async_computation | async-start | bytes 262144 | tf_op jit(solution)/shard_map/all_to_all | solution.py:182
  21.2 0.0 copy-start.5
  21.2 0.0 copy-done.2
  21.3 0.0 collective-permute-done
  21.3 0.7 copy-done.5
  22.1 7.3 %collective-permute-start.1 = (bf16[128,512]{1,0:T(8,128)(2,1)S(1)}, bf16[128,512]{1,0:T(8,128)(2,1)S(1)}, u32[]{:S(2)}, u32[]{:S(2)}) collective-permute-start(bf16[128,512]{1,0:T(8,128)(2,1)S(1)} %pad_maximum_fusion.2), channel_id=1, source_target_pairs={{0,32},{8,40},{16,48},{24,56},{32,0},{40,8},{48,16},{56,24},{1,33}... | collective-permute-start | bytes 393224 | tf_op jit(solution)/shard_map/ppermute | solution.py:170
  29.3 0.0 all-to-all-done
  29.4 0.2 fusion.1
  29.6 0.7 broadcast_in_dim.32
  30.2 0.0 copy-start.4
  30.2 4.2 %all-to-all-start.1 = ((bf16[8,16,512]{2,1,0:T(8,128)(2,1)}), bf16[8,16,512]{2,1,0:T(8,128)(2,1)S(1)}, u32[]{:S(2)}, u32[]{:S(2)}) async-start(bf16[8,16,512]{2,1,0:T(8,128)(2,1)} %broadcast_in_dim.32), calls=%async_computation.1 | async-start | bytes 262144 | tf_op jit(solution)/shard_map/all_to_all | solution.py:182
  34.4 0.0 collective-permute-done.1
  34.4 0.0 copy-start.1
  34.4 0.0 copy-start.3
  34.4 0.0 copy-start
  34.5 2.3 %collective-permute-start.3 = (bf16[256,512]{1,0:T(8,128)(2,1)S(1)}, bf16[256,512]{1,0:T(8,128)(2,1)S(1)}, u32[]{:S(2)}, u32[]{:S(2)}) collective-permute-start(bf16[256,512]{1,0:T(8,128)(2,1)S(1)} %pad_maximum_fusion.1), channel_id=1, source_target_pairs={{56,0},{0,8},{8,16},{16,24},{24,32},{32,40},{40,48},{48,56},{57,1}... | collective-permute-start | bytes 786440 | tf_op jit(solution)/shard_map/ppermute | solution.py:174
  36.8 5.2 %collective-permute-start.2 = (bf16[256,512]{1,0:T(8,128)(2,1)S(1)}, bf16[256,512]{1,0:T(8,128)(2,1)S(1)}, u32[]{:S(2)}, u32[]{:S(2)}) collective-permute-start(bf16[256,512]{1,0:T(8,128)(2,1)S(1)} %pad_maximum_fusion.1), channel_id=1, source_target_pairs={{16,0},{24,8},{32,16},{40,24},{48,32},{56,40},{0,48},{8,56},{17,1}... | collective-permute-start | bytes 786440 | tf_op jit(solution)/shard_map/ppermute | solution.py:174
  42.0 1.9 %all-to-all-done.1 = bf16[8,16,512]{2,1,0:T(8,128)(2,1)S(1)} async-done(((bf16[8,16,512]{2,1,0:T(8,128)(2,1)}), bf16[8,16,512]{2,1,0:T(8,128)(2,1)S(1)}, u32[]{:S(2)}, u32[]{:S(2)}) %all-to-all-start.1) | async-done | bytes 131104 | tf_op jit(solution)/shard_map/all_to_all | solution.py:182
  43.9 0.1 multiply_reduce_fusion
  44.0 0.0 copy-done.4
  44.0 0.0 copy-done.1
  44.0 0.0 copy-done.3
  44.0 0.0 copy-done
  44.1 2.9 %gated_rows.1 = bf16[2,4,128,512]{3,2,1,0:T(8,128)(2,1)} custom-call(bf16[256,512]{1,0:T(8,128)(2,1)S(1)} %copy-done.4, bf16[256,512]{1,0:T(8,128)(2,1)S(1)} %copy-done, bf16[256,512]{1,0:T(8,128)(2,1)S(1)} %copy-done.1, f32[16,512]{1,0:T(8,128)S(1)} %bitcast.17, f32[18,8,512]{2,1,0:T(8,128)S(1)} %copy-done.3, f32[16,512]{1,0:T(8,128)S(1)} %multiply_add_fusion.before_ref), custom_call_target="tpu_custom_call" | custom-call | tf_op jit(solution)/shard_map/gated_rows/pallas_call | solution.py:108
  47.0 7.4 %all-to-all-start.2 = ((bf16[8,128,512]{2,1,0:T(8,128)(2,1)}), bf16[8,128,512]{2,1,0:T(8,128)(2,1)S(1)}, u32[]{:S(2)}, u32[]{:S(2)}) async-start(bf16[8,128,512]{2,1,0:T(8,128)(2,1)} %bitcast.6), calls=%async_computation.2 | async-start | bytes 2097152 | tf_op jit(solution)/shard_map/all_to_all | solution.py:182
  54.3 1.9 %collective-permute-start.4 = (bf16[256,512]{1,0:T(8,128)(2,1)S(1)}, bf16[256,512]{1,0:T(8,128)(2,1)S(1)}, u32[]{:S(2)}, u32[]{:S(2)}) collective-permute-start(bf16[256,512]{1,0:T(8,128)(2,1)S(1)} %pad_maximum_fusion.1), channel_id=1, source_target_pairs={{8,0},{16,8},{24,16},{32,24},{40,32},{48,40},{56,48},{0,56},{9,1},... | collective-permute-start | bytes 786440 | tf_op jit(solution)/shard_map/ppermute | solution.py:174
  56.2 0.0 collective-permute-done.2
  56.3 2.0 %collective-permute-start.5 = (bf16[512,512]{1,0:T(8,128)(2,1)S(1)}, bf16[512,512]{1,0:T(8,128)(2,1)S(1)}, u32[]{:S(2)}, u32[]{:S(2)}) collective-permute-start(bf16[512,512]{1,0:T(8,128)(2,1)S(1)} %pad_maximum_fusion.own_low), channel_id=1, source_target_pairs={{0,1},{1,0},{2,3},{3,2},{4,5},{5,4},{6,7},{7,6},{8,9},{9,8},{10,11... | collective-permute-start | bytes 1572872 | tf_op jit(solution)/shard_map/ppermute | solution.py:170
  58.3 0.0 collective-permute-done.3
  58.3 5.7 %collective-permute-done.4 = bf16[256,512]{1,0:T(8,128)(2,1)S(1)} collective-permute-done((bf16[256,512]{1,0:T(8,128)(2,1)S(1)}, bf16[256,512]{1,0:T(8,128)(2,1)S(1)}, u32[]{:S(2)}, u32[]{:S(2)}) %collective-permute-start.4) | collective-permute-done | bytes 262176 | tf_op jit(solution)/shard_map/ppermute | solution.py:174
  64.1 2.8 %collective-permute-start.6 = (bf16[512,512]{1,0:T(8,128)(2,1)S(1)}, bf16[512,512]{1,0:T(8,128)(2,1)S(1)}, u32[]{:S(2)}, u32[]{:S(2)}) collective-permute-start(bf16[512,512]{1,0:T(8,128)(2,1)S(1)} %constant_dynamic-update-slice_fusion.own_high), channel_id=1, source_target_pairs={{0,1},{1,0},{2,3},{3,2},{4,5},{5,4},{6,7},{7,6},{8,9},{9,8},{10,11... | collective-permute-start | bytes 1572872 | tf_op jit(solution)/shard_map/ppermute | solution.py:170
  66.9 0.1 pad_add_fusion.place_ref
  67.0 0.0 collective-permute-done.5.other_low
  67.0 1.4 %collective-permute-done.6.other_high = bf16[512,512]{1,0:T(8,128)(2,1)S(1)} collective-permute-done((bf16[512,512]{1,0:T(8,128)(2,1)S(1)}, bf16[512,512]{1,0:T(8,128)(2,1)S(1)}, u32[]{:S(2)}, u32[]{:S(2)}) %collective-permute-start.6) | collective-permute-done | bytes 524320 | tf_op jit(solution)/shard_map/ppermute | solution.py:170
  68.4 0.9 all-to-all-done.2
  69.3 1.9 %project.1 = bf16[4,4,32,1024]{3,2,1,0:T(8,128)(2,1)S(1)} custom-call(s32[3]{0:T(128)S(1)} %pad_add_fusion.place_ref, bf16[2,512,512]{2,1,0:T(8,128)(2,1)S(1)} %bitcast.13, bf16[512,512]{1,0:T(8,128)(2,1)S(1)} %pad_maximum_fusion.own_low, bf16[512,512]{1,0:T(8,128)(2,1)S(1)} %constant_dynamic-update-slice_fusion.own_high, ...), custom_call_target="tpu_custom_call" | custom-call | tf_op jit(solution)/shard_map/project/pallas_call | solution.py:140
  71.2 30.7 %all_to_all.20 = bf16[16,32,1024]{2,1,0:T(8,128)(2,1)S(1)} all-to-all(bf16[16,32,1024]{2,1,0:T(8,128)(2,1)S(1)} %bitcast.14), channel_id=1, replica_groups=mesh['x'=4,'h'=2,'y'=8,'z'=4,'c'=2] {'z','x'}, dimensions={0} | all-to-all | bytes 2097152 | tf_op jit(solution)/shard_map/all_to_all | solution.py:182
  101.9 0.8 finish.1
  (11 shorter events, 0.2 us)
Async XLA Ops:
  0.0 21.3 %collective-permute-start = (bf16[64,512]{1,0:T(8,128)(2,1)}, bf16[64,512]{1,0:T(8,128)(2,1)S(1)}, u32[]{:S(2)}, u32[]{:S(2)}) collective-permute-start(bf16[64,512]{1,0:T(8,128)(2,1)} %bitcast.18), channel_id=1, source_target_pairs={{0,64},{64,0},{1,65},{65,1},{2,66},{66,2},{3,67},{67,3},{4,68},{68... | collective-permute-start | bytes 196616 | tf_op jit(solution)/shard_map/ppermute | solution.py:170
  14.2 7.0 %copy-start.2 = (f32[512,16]{0,1:T(8,128)S(1)}, f32[512,16]{0,1:T(8,128)}, u32[]{:S(2)}) copy-start(f32[512,16]{0,1:T(8,128)} %param.9) | copy-start | bytes 98308
  14.2 15.1 %all-to-all-start = ((bf16[8,16,512]{2,1,0:T(8,128)(2,1)}), bf16[8,16,512]{2,1,0:T(8,128)(2,1)S(1)}, u32[]{:S(2)}, u32[]{:S(2)}) async-start(bf16[8,16,512]{2,1,0:T(8,128)(2,1)} %get-tuple-element.10), calls=%async_computation | async-start | bytes 262144 | tf_op jit(solution)/shard_map/all_to_all | solution.py:182
  21.2 0.8 copy-start.5
  22.1 12.3 %collective-permute-start.1 = (bf16[128,512]{1,0:T(8,128)(2,1)S(1)}, bf16[128,512]{1,0:T(8,128)(2,1)S(1)}, u32[]{:S(2)}, u32[]{:S(2)}) collective-permute-start(bf16[128,512]{1,0:T(8,128)(2,1)S(1)} %pad_maximum_fusion.2), channel_id=1, source_target_pairs={{0,32},{8,40},{16,48},{24,56},{32,0},{40,8},{48,16},{56,24},{1,33}... | collective-permute-start | bytes 393224 | tf_op jit(solution)/shard_map/ppermute | solution.py:170
  30.2 13.8 %copy-start.4 = (bf16[256,512]{1,0:T(8,128)(2,1)S(1)}, bf16[256,512]{1,0:T(8,128)(2,1)}, u32[]{:S(2)}) copy-start(bf16[256,512]{1,0:T(8,128)(2,1)} %gate_ref.1) | copy-start | bytes 786436
  30.2 13.6 %all-to-all-start.1 = ((bf16[8,16,512]{2,1,0:T(8,128)(2,1)}), bf16[8,16,512]{2,1,0:T(8,128)(2,1)S(1)}, u32[]{:S(2)}, u32[]{:S(2)}) async-start(bf16[8,16,512]{2,1,0:T(8,128)(2,1)} %broadcast_in_dim.32), calls=%async_computation.1 | async-start | bytes 262144 | tf_op jit(solution)/shard_map/all_to_all | solution.py:182
  34.4 9.6 %copy-start.1 = (bf16[256,512]{1,0:T(8,128)(2,1)S(1)}, bf16[256,512]{1,0:T(8,128)(2,1)}, u32[]{:S(2)}) copy-start(bf16[256,512]{1,0:T(8,128)(2,1)} %value_ref.3) | copy-start | bytes 786436
  34.4 9.6 %copy-start.3 = (f32[18,8,512]{2,1,0:T(8,128)S(1)}, f32[18,8,512]{2,1,0:T(8,128)}, u32[]{:S(2)}) copy-start(f32[18,8,512]{2,1,0:T(8,128)} %get-tuple-element.9.runs_ref) | copy-start | bytes 884740
  34.4 9.6 %copy-start = (bf16[256,512]{1,0:T(8,128)(2,1)S(1)}, bf16[256,512]{1,0:T(8,128)(2,1)}, u32[]{:S(2)}) copy-start(bf16[256,512]{1,0:T(8,128)(2,1)} %key_ref.3) | copy-start | bytes 786436
  34.5 23.9 %collective-permute-start.3 = (bf16[256,512]{1,0:T(8,128)(2,1)S(1)}, bf16[256,512]{1,0:T(8,128)(2,1)S(1)}, u32[]{:S(2)}, u32[]{:S(2)}) collective-permute-start(bf16[256,512]{1,0:T(8,128)(2,1)S(1)} %pad_maximum_fusion.1), channel_id=1, source_target_pairs={{56,0},{0,8},{8,16},{16,24},{24,32},{32,40},{40,48},{48,56},{57,1}... | collective-permute-start | bytes 786440 | tf_op jit(solution)/shard_map/ppermute | solution.py:174
  36.8 19.5 %collective-permute-start.2 = (bf16[256,512]{1,0:T(8,128)(2,1)S(1)}, bf16[256,512]{1,0:T(8,128)(2,1)S(1)}, u32[]{:S(2)}, u32[]{:S(2)}) collective-permute-start(bf16[256,512]{1,0:T(8,128)(2,1)S(1)} %pad_maximum_fusion.1), channel_id=1, source_target_pairs={{16,0},{24,8},{32,16},{40,24},{48,32},{56,40},{0,48},{8,56},{17,1}... | collective-permute-start | bytes 786440 | tf_op jit(solution)/shard_map/ppermute | solution.py:174
  47.0 22.4 %all-to-all-start.2 = ((bf16[8,128,512]{2,1,0:T(8,128)(2,1)}), bf16[8,128,512]{2,1,0:T(8,128)(2,1)S(1)}, u32[]{:S(2)}, u32[]{:S(2)}) async-start(bf16[8,128,512]{2,1,0:T(8,128)(2,1)} %bitcast.6), calls=%async_computation.2 | async-start | bytes 2097152 | tf_op jit(solution)/shard_map/all_to_all | solution.py:182
  54.3 9.7 %collective-permute-start.4 = (bf16[256,512]{1,0:T(8,128)(2,1)S(1)}, bf16[256,512]{1,0:T(8,128)(2,1)S(1)}, u32[]{:S(2)}, u32[]{:S(2)}) collective-permute-start(bf16[256,512]{1,0:T(8,128)(2,1)S(1)} %pad_maximum_fusion.1), channel_id=1, source_target_pairs={{8,0},{16,8},{24,16},{32,24},{40,32},{48,40},{56,48},{0,56},{9,1},... | collective-permute-start | bytes 786440 | tf_op jit(solution)/shard_map/ppermute | solution.py:174
  56.3 10.7 %collective-permute-start.5 = (bf16[512,512]{1,0:T(8,128)(2,1)S(1)}, bf16[512,512]{1,0:T(8,128)(2,1)S(1)}, u32[]{:S(2)}, u32[]{:S(2)}) collective-permute-start(bf16[512,512]{1,0:T(8,128)(2,1)S(1)} %pad_maximum_fusion.own_low), channel_id=1, source_target_pairs={{0,1},{1,0},{2,3},{3,2},{4,5},{5,4},{6,7},{7,6},{8,9},{9,8},{10,11... | collective-permute-start | bytes 1572872 | tf_op jit(solution)/shard_map/ppermute | solution.py:170
  64.1 4.3 %collective-permute-start.6 = (bf16[512,512]{1,0:T(8,128)(2,1)S(1)}, bf16[512,512]{1,0:T(8,128)(2,1)S(1)}, u32[]{:S(2)}, u32[]{:S(2)}) collective-permute-start(bf16[512,512]{1,0:T(8,128)(2,1)S(1)} %constant_dynamic-update-slice_fusion.own_high), channel_id=1, source_target_pairs={{0,1},{1,0},{2,3},{3,2},{4,5},{5,4},{6,7},{7,6},{8,9},{9,8},{10,11... | collective-permute-start | bytes 1572872 | tf_op jit(solution)/shard_map/ppermute | solution.py:170

commit v5 on v4

--- a/solution.py
+++ b/solution.py
@@ -23,7 +23,7 @@
         at = pl.ds(r, SUB)
         runs_ref[poles + r // SUB] = residue_ref[at, :] * jnp.sqrt(rate_ref[at, :])
     steps = key_ref.shape[0] // SUB
-    later = (SUB - 1 - lax.broadcasted_iota(jnp.int32, (SUB, LANES), 0)).astype(f32) * steps
+    later = SUB - 1 - lax.broadcasted_iota(jnp.int32, (SUB, LANES), 0)
     for tile in range(chans // LANES):
         lanes = pl.ds(tile * LANES, LANES)
         signal[...] = key_ref[:, lanes].astype(f32) * value_ref[:, lanes].astype(f32)
@@ -34,11 +34,15 @@
             x = signal[pl.ds(j, SUB, stride=steps), :]
             return tuple(d * s + x for d, s in zip(decays, states))
 
-        states = lax.fori_loop(0, steps, step, (jnp.zeros((SUB, LANES), f32),) * poles, unroll=8)
+        states = lax.fori_loop(0, steps, step, (jnp.zeros((SUB, LANES), f32),) * poles, unroll=True)
         ends = []
         for r in range(poles):
             runs_ref[r, :, lanes] = states[r]
-            ends.append(jnp.sum(states[r] * jnp.exp(-rates[r] * later), axis=0, keepdims=True))
+            fade, faded = jnp.exp(-rates[r] * steps), states[r]
+            for runs in (1, 2, 4):
+                faded = jnp.where(later // runs % 2 == 1, fade * faded, faded)
+                fade = fade * fade
+            ends.append(jnp.sum(faded, axis=0, keepdims=True))
         ends = jnp.concatenate(ends, axis=0).astype(block_ref.dtype)
         for copy in range(block_ref.shape[0]):
             block_ref[copy, :, lanes] = ends

time: 104 us -> 104 us (level)
  transfers between devices with their start and end apart: 10 -> 10, of which waited for: 4 -> 4; matrix products, arithmetic and copies ran while one was open for 1% -> 1% of each run, Pallas kernels for 6% -> 5%
where the time goes in v5:
time: 104 us; the launch traced here: 103 us
  starting transfers between devices  51.4 us (49%)
  blocking collectives  30.7 us (30%)
  waiting for transfers between devices  9.96 us (10%)
  Pallas kernels  8.34 us (8%)
  local copies, waits for them, and re-layouts  1.46 us (1%)
    all_to_all x1, blocking collectives, exchange(): return lax.all_to_all(array, axes, 0, 0, tiled=True)  30.7 us
    ppermute x4, starting transfers between devices, swap(): lax.ppermute(array, axis, [(i, i ^ bit) for i in range(dict(AXES)[axis])])  23.5 us
    all_to_all x3, starting transfers between devices, exchange(): return lax.all_to_all(array, axes, 0, 0, tiled=True)  18.5 us
    ppermute x3, starting transfers between devices, from_along_y(): return lax.ppermute(array, 'y', [((i + step) % NY, i) for i in range(NY)])  9.42 us
    ppermute x3, waiting for transfers between devices, from_along_y(): return lax.ppermute(array, 'y', [((i + step) % NY, i) for i in range(NY)])  5.73 us
    pallas_call x1, Pallas kernels, gated_rows(): pl.pallas_call(gated_kernel, out_shape=jax.ShapeDtypeStruct((NC, NX, leng...  2.9 us
    all_to_all x3, waiting for transfers between devices, exchange(): return lax.all_to_all(array, axes, 0, 0, tiled=True)  2.79 us
    pallas_call x1, Pallas kernels, run_states(): pl.pallas_call(run_states_kernel, out_shape=(jax.ShapeDtypeStruct((poles...  2.7 us
  transfers between devices with their start and end apart: 10, of which 4 were waited for; matrix products, arithmetic and copies ran while one was open for 1% of the time, Pallas kernels for 5%

profile of v5, /device:TPU:1, one launch (start us, length us, event | category | flops | bytes accessed | tf_op | source)
XLA Modules:
  0.0 102.7 jit_solution(14341907867913341913)
XLA Ops:
  0.0 11.5 %collective-permute-start = (bf16[64,512]{1,0:T(8,128)(2,1)}, bf16[64,512]{1,0:T(8,128)(2,1)S(1)}, u32[]{:S(2)}, u32[]{:S(2)}) collective-permute-start(bf16[64,512]{1,0:T(8,128)(2,1)} %bitcast.18), channel_id=1, source_target_pairs={{0,64},{64,0},{1,65},{65,1},{2,66},{66,2},{3,67},{67,3},{4,68},{68... | collective-permute-start | bytes 196616 | tf_op jit(solution)/shard_map/ppermute | solution.py:174
  11.5 2.7 %run_states.1 = (f32[18,8,512]{2,1,0:T(8,128)}, bf16[8,16,512]{2,1,0:T(8,128)(2,1)}) custom-call(bf16[256,512]{1,0:T(8,128)(2,1)} %key_ref.3, bf16[256,512]{1,0:T(8,128)(2,1)} %value_ref.3, f32[16,512]{1,0:T(8,128)} %bitcast.16, f32[16,512]{1,0:T(8,128)} %bitcast.22), custom_call_target="tpu_custom_call" | custom-call | tf_op jit(solution)/shard_map/run_states/pallas_call | solution.py:53
  14.2 0.0 copy-start.2
  14.2 7.0 %all-to-all-start = ((bf16[8,16,512]{2,1,0:T(8,128)(2,1)}), bf16[8,16,512]{2,1,0:T(8,128)(2,1)S(1)}, u32[]{:S(2)}, u32[]{:S(2)}) async-start(bf16[8,16,512]{2,1,0:T(8,128)(2,1)} %get-tuple-element.10), calls=%async_computation | async-start | bytes 262144 | tf_op jit(solution)/shard_map/all_to_all | solution.py:186
  21.1 0.0 copy-start.5
  21.1 0.0 copy-done.2
  21.2 0.0 collective-permute-done
  21.2 0.7 copy-done.5
  22.0 7.3 %collective-permute-start.1 = (bf16[128,512]{1,0:T(8,128)(2,1)S(1)}, bf16[128,512]{1,0:T(8,128)(2,1)S(1)}, u32[]{:S(2)}, u32[]{:S(2)}) collective-permute-start(bf16[128,512]{1,0:T(8,128)(2,1)S(1)} %pad_maximum_fusion.2), channel_id=1, source_target_pairs={{0,32},{8,40},{16,48},{24,56},{32,0},{40,8},{48,16},{56,24},{1,33}... | collective-permute-start | bytes 393224 | tf_op jit(solution)/shard_map/ppermute | solution.py:174
  29.3 0.0 all-to-all-done
  29.3 0.2 fusion.1
  29.5 0.7 broadcast_in_dim.32
  30.1 0.0 copy-start.4
  30.1 4.2 %all-to-all-start.1 = ((bf16[8,16,512]{2,1,0:T(8,128)(2,1)}), bf16[8,16,512]{2,1,0:T(8,128)(2,1)S(1)}, u32[]{:S(2)}, u32[]{:S(2)}) async-start(bf16[8,16,512]{2,1,0:T(8,128)(2,1)} %broadcast_in_dim.32), calls=%async_computation.1 | async-start | bytes 262144 | tf_op jit(solution)/shard_map/all_to_all | solution.py:186
  34.3 0.0 collective-permute-done.1
  34.3 0.0 copy-start.1
  34.3 0.0 copy-start.3
  34.4 0.0 copy-start
  34.4 2.3 %collective-permute-start.3 = (bf16[256,512]{1,0:T(8,128)(2,1)S(1)}, bf16[256,512]{1,0:T(8,128)(2,1)S(1)}, u32[]{:S(2)}, u32[]{:S(2)}) collective-permute-start(bf16[256,512]{1,0:T(8,128)(2,1)S(1)} %pad_maximum_fusion.1), channel_id=1, source_target_pairs={{56,0},{0,8},{8,16},{16,24},{24,32},{32,40},{40,48},{48,56},{57,1}... | collective-permute-start | bytes 786440 | tf_op jit(solution)/shard_map/ppermute | solution.py:178
  36.7 5.2 %collective-permute-start.2 = (bf16[256,512]{1,0:T(8,128)(2,1)S(1)}, bf16[256,512]{1,0:T(8,128)(2,1)S(1)}, u32[]{:S(2)}, u32[]{:S(2)}) collective-permute-start(bf16[256,512]{1,0:T(8,128)(2,1)S(1)} %pad_maximum_fusion.1), channel_id=1, source_target_pairs={{16,0},{24,8},{32,16},{40,24},{48,32},{56,40},{0,48},{8,56},{17,1}... | collective-permute-start | bytes 786440 | tf_op jit(solution)/shard_map/ppermute | solution.py:178
  41.9 1.9 %all-to-all-done.1 = bf16[8,16,512]{2,1,0:T(8,128)(2,1)S(1)} async-done(((bf16[8,16,512]{2,1,0:T(8,128)(2,1)}), bf16[8,16,512]{2,1,0:T(8,128)(2,1)S(1)}, u32[]{:S(2)}, u32[]{:S(2)}) %all-to-all-start.1) | async-done | bytes 131104 | tf_op jit(solution)/shard_map/all_to_all | solution.py:186
  43.8 0.1 multiply_reduce_fusion
  43.9 0.0 copy-done.4
  43.9 0.0 copy-done.1
  44.0 0.0 copy-done.3
  44.0 0.0 copy-done
  44.0 2.9 %gated_rows.1 = bf16[2,4,128,512]{3,2,1,0:T(8,128)(2,1)} custom-call(bf16[256,512]{1,0:T(8,128)(2,1)S(1)} %copy-done.4, bf16[256,512]{1,0:T(8,128)(2,1)S(1)} %copy-done, bf16[256,512]{1,0:T(8,128)(2,1)S(1)} %copy-done.1, f32[16,512]{1,0:T(8,128)S(1)} %bitcast.17, f32[18,8,512]{2,1,0:T(8,128)S(1)} %copy-done.3, f32[16,512]{1,0:T(8,128)S(1)} %multiply_add_fusion.before_ref), custom_call_target="tpu_custom_call" | custom-call | tf_op jit(solution)/shard_map/gated_rows/pallas_call | solution.py:112
  46.9 7.4 %all-to-all-start.2 = ((bf16[8,128,512]{2,1,0:T(8,128)(2,1)}), bf16[8,128,512]{2,1,0:T(8,128)(2,1)S(1)}, u32[]{:S(2)}, u32[]{:S(2)}) async-start(bf16[8,128,512]{2,1,0:T(8,128)(2,1)} %bitcast.6), calls=%async_computation.2 | async-start | bytes 2097152 | tf_op jit(solution)/shard_map/all_to_all | solution.py:186
  54.2 1.9 %collective-permute-start.4 = (bf16[256,512]{1,0:T(8,128)(2,1)S(1)}, bf16[256,512]{1,0:T(8,128)(2,1)S(1)}, u32[]{:S(2)}, u32[]{:S(2)}) collective-permute-start(bf16[256,512]{1,0:T(8,128)(2,1)S(1)} %pad_maximum_fusion.1), channel_id=1, source_target_pairs={{8,0},{16,8},{24,16},{32,24},{40,32},{48,40},{56,48},{0,56},{9,1},... | collective-permute-start | bytes 786440 | tf_op jit(solution)/shard_map/ppermute | solution.py:178
  56.2 0.0 collective-permute-done.2
  56.2 2.0 %collective-permute-start.5 = (bf16[512,512]{1,0:T(8,128)(2,1)S(1)}, bf16[512,512]{1,0:T(8,128)(2,1)S(1)}, u32[]{:S(2)}, u32[]{:S(2)}) collective-permute-start(bf16[512,512]{1,0:T(8,128)(2,1)S(1)} %pad_maximum_fusion.own_low), channel_id=1, source_target_pairs={{0,1},{1,0},{2,3},{3,2},{4,5},{5,4},{6,7},{7,6},{8,9},{9,8},{10,11... | collective-permute-start | bytes 1572872 | tf_op jit(solution)/shard_map/ppermute | solution.py:174
  58.2 0.0 collective-permute-done.3
  58.3 5.7 %collective-permute-done.4 = bf16[256,512]{1,0:T(8,128)(2,1)S(1)} collective-permute-done((bf16[256,512]{1,0:T(8,128)(2,1)S(1)}, bf16[256,512]{1,0:T(8,128)(2,1)S(1)}, u32[]{:S(2)}, u32[]{:S(2)}) %collective-permute-start.4) | collective-permute-done | bytes 262176 | tf_op jit(solution)/shard_map/ppermute | solution.py:178
  64.0 2.8 %collective-permute-start.6 = (bf16[512,512]{1,0:T(8,128)(2,1)S(1)}, bf16[512,512]{1,0:T(8,128)(2,1)S(1)}, u32[]{:S(2)}, u32[]{:S(2)}) collective-permute-start(bf16[512,512]{1,0:T(8,128)(2,1)S(1)} %constant_dynamic-update-slice_fusion.own_high), channel_id=1, source_target_pairs={{0,1},{1,0},{2,3},{3,2},{4,5},{5,4},{6,7},{7,6},{8,9},{9,8},{10,11... | collective-permute-start | bytes 1572872 | tf_op jit(solution)/shard_map/ppermute | solution.py:174
  66.8 0.1 pad_add_fusion.place_ref
  66.9 0.0 collective-permute-done.5.other_low
  66.9 1.4 %collective-permute-done.6.other_high = bf16[512,512]{1,0:T(8,128)(2,1)S(1)} collective-permute-done((bf16[512,512]{1,0:T(8,128)(2,1)S(1)}, bf16[512,512]{1,0:T(8,128)(2,1)S(1)}, u32[]{:S(2)}, u32[]{:S(2)}) %collective-permute-start.6) | collective-permute-done | bytes 524320 | tf_op jit(solution)/shard_map/ppermute | solution.py:174
  68.3 0.9 all-to-all-done.2
  69.2 1.9 %project.1 = bf16[4,4,32,1024]{3,2,1,0:T(8,128)(2,1)S(1)} custom-call(s32[3]{0:T(128)S(1)} %pad_add_fusion.place_ref, bf16[2,512,512]{2,1,0:T(8,128)(2,1)S(1)} %bitcast.13, bf16[512,512]{1,0:T(8,128)(2,1)S(1)} %pad_maximum_fusion.own_low, bf16[512,512]{1,0:T(8,128)(2,1)S(1)} %constant_dynamic-update-slice_fusion.own_high, ...), custom_call_target="tpu_custom_call" | custom-call | tf_op jit(solution)/shard_map/project/pallas_call | solution.py:144
  71.1 30.7 %all_to_all.20 = bf16[16,32,1024]{2,1,0:T(8,128)(2,1)S(1)} all-to-all(bf16[16,32,1024]{2,1,0:T(8,128)(2,1)S(1)} %bitcast.14), channel_id=1, replica_groups=mesh['x'=4,'h'=2,'y'=8,'z'=4,'c'=2] {'z','x'}, dimensions={0} | all-to-all | bytes 2097152 | tf_op jit(solution)/shard_map/all_to_all | solution.py:186
  101.9 0.8 finish.1
  (11 shorter events, 0.2 us)
Async XLA Ops:
  0.0 21.2 %collective-permute-start = (bf16[64,512]{1,0:T(8,128)(2,1)}, bf16[64,512]{1,0:T(8,128)(2,1)S(1)}, u32[]{:S(2)}, u32[]{:S(2)}) collective-permute-start(bf16[64,512]{1,0:T(8,128)(2,1)} %bitcast.18), channel_id=1, source_target_pairs={{0,64},{64,0},{1,65},{65,1},{2,66},{66,2},{3,67},{67,3},{4,68},{68... | collective-permute-start | bytes 196616 | tf_op jit(solution)/shard_map/ppermute | solution.py:174
  14.2 7.0 %copy-start.2 = (f32[512,16]{0,1:T(8,128)S(1)}, f32[512,16]{0,1:T(8,128)}, u32[]{:S(2)}) copy-start(f32[512,16]{0,1:T(8,128)} %param.9) | copy-start | bytes 98308
  14.2 15.1 %all-to-all-start = ((bf16[8,16,512]{2,1,0:T(8,128)(2,1)}), bf16[8,16,512]{2,1,0:T(8,128)(2,1)S(1)}, u32[]{:S(2)}, u32[]{:S(2)}) async-start(bf16[8,16,512]{2,1,0:T(8,128)(2,1)} %get-tuple-element.10), calls=%async_computation | async-start | bytes 262144 | tf_op jit(solution)/shard_map/all_to_all | solution.py:186
  21.1 0.8 copy-start.5
  22.0 12.3 %collective-permute-start.1 = (bf16[128,512]{1,0:T(8,128)(2,1)S(1)}, bf16[128,512]{1,0:T(8,128)(2,1)S(1)}, u32[]{:S(2)}, u32[]{:S(2)}) collective-permute-start(bf16[128,512]{1,0:T(8,128)(2,1)S(1)} %pad_maximum_fusion.2), channel_id=1, source_target_pairs={{0,32},{8,40},{16,48},{24,56},{32,0},{40,8},{48,16},{56,24},{1,33}... | collective-permute-start | bytes 393224 | tf_op jit(solution)/shard_map/ppermute | solution.py:174
  30.1 13.8 %copy-start.4 = (bf16[256,512]{1,0:T(8,128)(2,1)S(1)}, bf16[256,512]{1,0:T(8,128)(2,1)}, u32[]{:S(2)}) copy-start(bf16[256,512]{1,0:T(8,128)(2,1)} %gate_ref.1) | copy-start | bytes 786436
  30.1 13.6 %all-to-all-start.1 = ((bf16[8,16,512]{2,1,0:T(8,128)(2,1)}), bf16[8,16,512]{2,1,0:T(8,128)(2,1)S(1)}, u32[]{:S(2)}, u32[]{:S(2)}) async-start(bf16[8,16,512]{2,1,0:T(8,128)(2,1)} %broadcast_in_dim.32), calls=%async_computation.1 | async-start | bytes 262144 | tf_op jit(solution)/shard_map/all_to_all | solution.py:186
  34.3 9.6 %copy-start.1 = (bf16[256,512]{1,0:T(8,128)(2,1)S(1)}, bf16[256,512]{1,0:T(8,128)(2,1)}, u32[]{:S(2)}) copy-start(bf16[256,512]{1,0:T(8,128)(2,1)} %value_ref.3) | copy-start | bytes 786436
  34.3 9.6 %copy-start.3 = (f32[18,8,512]{2,1,0:T(8,128)S(1)}, f32[18,8,512]{2,1,0:T(8,128)}, u32[]{:S(2)}) copy-start(f32[18,8,512]{2,1,0:T(8,128)} %get-tuple-element.9.runs_ref) | copy-start | bytes 884740
  34.4 9.6 %copy-start = (bf16[256,512]{1,0:T(8,128)(2,1)S(1)}, bf16[256,512]{1,0:T(8,128)(2,1)}, u32[]{:S(2)}) copy-start(bf16[256,512]{1,0:T(8,128)(2,1)} %key_ref.3) | copy-start | bytes 786436
  34.4 23.9 %collective-permute-start.3 = (bf16[256,512]{1,0:T(8,128)(2,1)S(1)}, bf16[256,512]{1,0:T(8,128)(2,1)S(1)}, u32[]{:S(2)}, u32[]{:S(2)}) collective-permute-start(bf16[256,512]{1,0:T(8,128)(2,1)S(1)} %pad_maximum_fusion.1), channel_id=1, source_target_pairs={{56,0},{0,8},{8,16},{16,24},{24,32},{32,40},{40,48},{48,56},{57,1}... | collective-permute-start | bytes 786440 | tf_op jit(solution)/shard_map/ppermute | solution.py:178
  36.7 19.5 %collective-permute-start.2 = (bf16[256,512]{1,0:T(8,128)(2,1)S(1)}, bf16[256,512]{1,0:T(8,128)(2,1)S(1)}, u32[]{:S(2)}, u32[]{:S(2)}) collective-permute-start(bf16[256,512]{1,0:T(8,128)(2,1)S(1)} %pad_maximum_fusion.1), channel_id=1, source_target_pairs={{16,0},{24,8},{32,16},{40,24},{48,32},{56,40},{0,48},{8,56},{17,1}... | collective-permute-start | bytes 786440 | tf_op jit(solution)/shard_map/ppermute | solution.py:178
  46.9 22.4 %all-to-all-start.2 = ((bf16[8,128,512]{2,1,0:T(8,128)(2,1)}), bf16[8,128,512]{2,1,0:T(8,128)(2,1)S(1)}, u32[]{:S(2)}, u32[]{:S(2)}) async-start(bf16[8,128,512]{2,1,0:T(8,128)(2,1)} %bitcast.6), calls=%async_computation.2 | async-start | bytes 2097152 | tf_op jit(solution)/shard_map/all_to_all | solution.py:186
  54.2 9.7 %collective-permute-start.4 = (bf16[256,512]{1,0:T(8,128)(2,1)S(1)}, bf16[256,512]{1,0:T(8,128)(2,1)S(1)}, u32[]{:S(2)}, u32[]{:S(2)}) collective-permute-start(bf16[256,512]{1,0:T(8,128)(2,1)S(1)} %pad_maximum_fusion.1), channel_id=1, source_target_pairs={{8,0},{16,8},{24,16},{32,24},{40,32},{48,40},{56,48},{0,56},{9,1},... | collective-permute-start | bytes 786440 | tf_op jit(solution)/shard_map/ppermute | solution.py:178
  56.2 10.7 %collective-permute-start.5 = (bf16[512,512]{1,0:T(8,128)(2,1)S(1)}, bf16[512,512]{1,0:T(8,128)(2,1)S(1)}, u32[]{:S(2)}, u32[]{:S(2)}) collective-permute-start(bf16[512,512]{1,0:T(8,128)(2,1)S(1)} %pad_maximum_fusion.own_low), channel_id=1, source_target_pairs={{0,1},{1,0},{2,3},{3,2},{4,5},{5,4},{6,7},{7,6},{8,9},{9,8},{10,11... | collective-permute-start | bytes 1572872 | tf_op jit(solution)/shard_map/ppermute | solution.py:174
  64.0 4.3 %collective-permute-start.6 = (bf16[512,512]{1,0:T(8,128)(2,1)S(1)}, bf16[512,512]{1,0:T(8,128)(2,1)S(1)}, u32[]{:S(2)}, u32[]{:S(2)}) collective-permute-start(bf16[512,512]{1,0:T(8,128)(2,1)S(1)} %constant_dynamic-update-slice_fusion.own_high), channel_id=1, source_target_pairs={{0,1},{1,0},{2,3},{3,2},{4,5},{5,4},{6,7},{7,6},{8,9},{9,8},{10,11... | collective-permute-start | bytes 1572872 | tf_op jit(solution)/shard_map/ppermute | solution.py:174

commit v6 on v4

--- a/solution.py
+++ b/solution.py
@@ -9,7 +9,7 @@
 NX, NH, NY, NZ, NC = (size for _, size in AXES)
 SEQ = ("x", "h", "y")
 CH = ("z", "c")
-RING = (2, -1, 1)
+RING = (-2, -1, 1)
 
 SUB = 8
 LANES = 128

time: 104 us -> 104 us (level)
  no operation moved by 1% of the time
where the time goes in v6:
time: 104 us; the launch traced here: 103 us
  starting transfers between devices  52.3 us (50%)
  blocking collectives  30.7 us (30%)
  waiting for transfers between devices  9.04 us (9%)
  Pallas kernels  8.42 us (8%)
  local copies, waits for them, and re-layouts  1.46 us (1%)
    all_to_all x1, blocking collectives, exchange(): return lax.all_to_all(array, axes, 0, 0, tiled=True)  30.7 us
    ppermute x4, starting transfers between devices, swap(): lax.ppermute(array, axis, [(i, i ^ bit) for i in range(dict(AXES)[axis])])  23.9 us
    all_to_all x3, starting transfers between devices, exchange(): return lax.all_to_all(array, axes, 0, 0, tiled=True)  18.5 us
    ppermute x3, starting transfers between devices, from_along_y(): return lax.ppermute(array, 'y', [((i + step) % NY, i) for i in range(NY)])  9.99 us
    ppermute x3, waiting for transfers between devices, from_along_y(): return lax.ppermute(array, 'y', [((i + step) % NY, i) for i in range(NY)])  5.38 us
    pallas_call x1, Pallas kernels, gated_rows(): pl.pallas_call(gated_kernel, out_shape=jax.ShapeDtypeStruct((NC, NX, leng...  2.9 us
    pallas_call x1, Pallas kernels, run_states(): pl.pallas_call(run_states_kernel, out_shape=(jax.ShapeDtypeStruct((poles...  2.78 us
    all_to_all x3, waiting for transfers between devices, exchange(): return lax.all_to_all(array, axes, 0, 0, tiled=True)  2.22 us
  transfers between devices with their start and end apart: 10, of which 4 were waited for; matrix products, arithmetic and copies ran while one was open for 1% of the time, Pallas kernels for 6%

profile of v6, /device:TPU:1, one launch (start us, length us, event | category | flops | bytes accessed | tf_op | source)
XLA Modules:
  0.0 102.8 jit_solution(11805894562634005212)
XLA Ops:
  0.0 11.5 %collective-permute-start = (bf16[64,512]{1,0:T(8,128)(2,1)}, bf16[64,512]{1,0:T(8,128)(2,1)S(1)}, u32[]{:S(2)}, u32[]{:S(2)}) collective-permute-start(bf16[64,512]{1,0:T(8,128)(2,1)} %bitcast.18), channel_id=1, source_target_pairs={{0,64},{64,0},{1,65},{65,1},{2,66},{66,2},{3,67},{67,3},{4,68},{68... | collective-permute-start | bytes 196616 | tf_op jit(solution)/shard_map/ppermute | solution.py:170
  11.5 2.8 %run_states.1 = (f32[18,8,512]{2,1,0:T(8,128)}, bf16[8,16,512]{2,1,0:T(8,128)(2,1)}) custom-call(bf16[256,512]{1,0:T(8,128)(2,1)} %key_ref.3, bf16[256,512]{1,0:T(8,128)(2,1)} %value_ref.3, f32[16,512]{1,0:T(8,128)} %bitcast.16, f32[16,512]{1,0:T(8,128)} %bitcast.22), custom_call_target="tpu_custom_call" | custom-call | tf_op jit(solution)/shard_map/run_states/pallas_call | solution.py:49
  14.2 0.0 copy-start.2
  14.2 7.0 %all-to-all-start = ((bf16[8,16,512]{2,1,0:T(8,128)(2,1)}), bf16[8,16,512]{2,1,0:T(8,128)(2,1)S(1)}, u32[]{:S(2)}, u32[]{:S(2)}) async-start(bf16[8,16,512]{2,1,0:T(8,128)(2,1)} %get-tuple-element.10), calls=%async_computation | async-start | bytes 262144 | tf_op jit(solution)/shard_map/all_to_all | solution.py:182
  21.2 0.0 copy-start.5
  21.2 0.0 copy-done.2
  21.3 0.0 collective-permute-done
  21.3 0.7 copy-done.5
  22.1 7.3 %collective-permute-start.1 = (bf16[128,512]{1,0:T(8,128)(2,1)S(1)}, bf16[128,512]{1,0:T(8,128)(2,1)S(1)}, u32[]{:S(2)}, u32[]{:S(2)}) collective-permute-start(bf16[128,512]{1,0:T(8,128)(2,1)S(1)} %pad_maximum_fusion.2), channel_id=1, source_target_pairs={{0,32},{8,40},{16,48},{24,56},{32,0},{40,8},{48,16},{56,24},{1,33}... | collective-permute-start | bytes 393224 | tf_op jit(solution)/shard_map/ppermute | solution.py:170
  29.3 0.0 all-to-all-done
  29.4 0.2 fusion.1
  29.6 0.7 broadcast_in_dim.32
  30.2 0.0 copy-start.4
  30.2 4.2 %all-to-all-start.1 = ((bf16[8,16,512]{2,1,0:T(8,128)(2,1)}), bf16[8,16,512]{2,1,0:T(8,128)(2,1)S(1)}, u32[]{:S(2)}, u32[]{:S(2)}) async-start(bf16[8,16,512]{2,1,0:T(8,128)(2,1)} %broadcast_in_dim.32), calls=%async_computation.1 | async-start | bytes 262144 | tf_op jit(solution)/shard_map/all_to_all | solution.py:182
  34.4 0.0 collective-permute-done.1
  34.4 0.0 copy-start.1
  34.4 0.0 copy-start.3
  34.4 0.0 copy-start
  34.5 2.3 %collective-permute-start.3 = (bf16[256,512]{1,0:T(8,128)(2,1)S(1)}, bf16[256,512]{1,0:T(8,128)(2,1)S(1)}, u32[]{:S(2)}, u32[]{:S(2)}) collective-permute-start(bf16[256,512]{1,0:T(8,128)(2,1)S(1)} %pad_maximum_fusion.1), channel_id=1, source_target_pairs={{56,0},{0,8},{8,16},{16,24},{24,32},{32,40},{40,48},{48,56},{57,1}... | collective-permute-start | bytes 786440 | tf_op jit(solution)/shard_map/ppermute | solution.py:174
  36.8 5.8 %collective-permute-start.2 = (bf16[256,512]{1,0:T(8,128)(2,1)S(1)}, bf16[256,512]{1,0:T(8,128)(2,1)S(1)}, u32[]{:S(2)}, u32[]{:S(2)}) collective-permute-start(bf16[256,512]{1,0:T(8,128)(2,1)S(1)} %pad_maximum_fusion.1), channel_id=1, source_target_pairs={{48,0},{56,8},{0,16},{8,24},{16,32},{24,40},{32,48},{40,56},{49,1}... | collective-permute-start | bytes 786440 | tf_op jit(solution)/shard_map/ppermute | solution.py:174
  42.6 1.3 %all-to-all-done.1 = bf16[8,16,512]{2,1,0:T(8,128)(2,1)S(1)} async-done(((bf16[8,16,512]{2,1,0:T(8,128)(2,1)}), bf16[8,16,512]{2,1,0:T(8,128)(2,1)S(1)}, u32[]{:S(2)}, u32[]{:S(2)}) %all-to-all-start.1) | async-done | bytes 131104 | tf_op jit(solution)/shard_map/all_to_all | solution.py:182
  43.9 0.1 multiply_reduce_fusion
  44.0 0.0 copy-done.4
  44.0 0.0 copy-done.1
  44.0 0.0 copy-done.3
  44.0 0.0 copy-done
  44.1 2.9 %gated_rows.1 = bf16[2,4,128,512]{3,2,1,0:T(8,128)(2,1)} custom-call(bf16[256,512]{1,0:T(8,128)(2,1)S(1)} %copy-done.4, bf16[256,512]{1,0:T(8,128)(2,1)S(1)} %copy-done, bf16[256,512]{1,0:T(8,128)(2,1)S(1)} %copy-done.1, f32[16,512]{1,0:T(8,128)S(1)} %bitcast.17, f32[18,8,512]{2,1,0:T(8,128)S(1)} %copy-done.3, f32[16,512]{1,0:T(8,128)S(1)} %multiply_add_fusion.before_ref), custom_call_target="tpu_custom_call" | custom-call | tf_op jit(solution)/shard_map/gated_rows/pallas_call | solution.py:108
  47.0 7.4 %all-to-all-start.2 = ((bf16[8,128,512]{2,1,0:T(8,128)(2,1)}), bf16[8,128,512]{2,1,0:T(8,128)(2,1)S(1)}, u32[]{:S(2)}, u32[]{:S(2)}) async-start(bf16[8,128,512]{2,1,0:T(8,128)(2,1)} %bitcast.6), calls=%async_computation.2 | async-start | bytes 2097152 | tf_op jit(solution)/shard_map/all_to_all | solution.py:182
  54.3 1.9 %collective-permute-start.4 = (bf16[256,512]{1,0:T(8,128)(2,1)S(1)}, bf16[256,512]{1,0:T(8,128)(2,1)S(1)}, u32[]{:S(2)}, u32[]{:S(2)}) collective-permute-start(bf16[256,512]{1,0:T(8,128)(2,1)S(1)} %pad_maximum_fusion.1), channel_id=1, source_target_pairs={{8,0},{16,8},{24,16},{32,24},{40,32},{48,40},{56,48},{0,56},{9,1},... | collective-permute-start | bytes 786440 | tf_op jit(solution)/shard_map/ppermute | solution.py:174
  56.2 0.0 collective-permute-done.2
  56.3 2.4 %collective-permute-start.5 = (bf16[512,512]{1,0:T(8,128)(2,1)S(1)}, bf16[512,512]{1,0:T(8,128)(2,1)S(1)}, u32[]{:S(2)}, u32[]{:S(2)}) collective-permute-start(bf16[512,512]{1,0:T(8,128)(2,1)S(1)} %pad_maximum_fusion.own_low), channel_id=1, source_target_pairs={{0,1},{1,0},{2,3},{3,2},{4,5},{5,4},{6,7},{7,6},{8,9},{9,8},{10,11... | collective-permute-start | bytes 1572872 | tf_op jit(solution)/shard_map/ppermute | solution.py:170
  58.7 0.0 collective-permute-done.3
  58.7 5.4 %collective-permute-done.4 = bf16[256,512]{1,0:T(8,128)(2,1)S(1)} collective-permute-done((bf16[256,512]{1,0:T(8,128)(2,1)S(1)}, bf16[256,512]{1,0:T(8,128)(2,1)S(1)}, u32[]{:S(2)}, u32[]{:S(2)}) %collective-permute-start.4) | collective-permute-done | bytes 262176 | tf_op jit(solution)/shard_map/ppermute | solution.py:174
  64.1 2.8 %collective-permute-start.6 = (bf16[512,512]{1,0:T(8,128)(2,1)S(1)}, bf16[512,512]{1,0:T(8,128)(2,1)S(1)}, u32[]{:S(2)}, u32[]{:S(2)}) collective-permute-start(bf16[512,512]{1,0:T(8,128)(2,1)S(1)} %constant_dynamic-update-slice_fusion.own_high), channel_id=1, source_target_pairs={{0,1},{1,0},{2,3},{3,2},{4,5},{5,4},{6,7},{7,6},{8,9},{9,8},{10,11... | collective-permute-start | bytes 1572872 | tf_op jit(solution)/shard_map/ppermute | solution.py:170
  66.9 0.1 pad_add_fusion.place_ref
  67.0 0.0 collective-permute-done.5.other_low
  67.0 1.4 %collective-permute-done.6.other_high = bf16[512,512]{1,0:T(8,128)(2,1)S(1)} collective-permute-done((bf16[512,512]{1,0:T(8,128)(2,1)S(1)}, bf16[512,512]{1,0:T(8,128)(2,1)S(1)}, u32[]{:S(2)}, u32[]{:S(2)}) %collective-permute-start.6) | collective-permute-done | bytes 524320 | tf_op jit(solution)/shard_map/ppermute | solution.py:170
  68.4 0.9 all-to-all-done.2
  69.3 1.9 %project.1 = bf16[4,4,32,1024]{3,2,1,0:T(8,128)(2,1)S(1)} custom-call(s32[3]{0:T(128)S(1)} %pad_add_fusion.place_ref, bf16[2,512,512]{2,1,0:T(8,128)(2,1)S(1)} %bitcast.13, bf16[512,512]{1,0:T(8,128)(2,1)S(1)} %pad_maximum_fusion.own_low, bf16[512,512]{1,0:T(8,128)(2,1)S(1)} %constant_dynamic-update-slice_fusion.own_high, ...), custom_call_target="tpu_custom_call" | custom-call | tf_op jit(solution)/shard_map/project/pallas_call | solution.py:140
  71.2 30.7 %all_to_all.20 = bf16[16,32,1024]{2,1,0:T(8,128)(2,1)S(1)} all-to-all(bf16[16,32,1024]{2,1,0:T(8,128)(2,1)S(1)} %bitcast.14), channel_id=1, replica_groups=mesh['x'=4,'h'=2,'y'=8,'z'=4,'c'=2] {'z','x'}, dimensions={0} | all-to-all | bytes 2097152 | tf_op jit(solution)/shard_map/all_to_all | solution.py:182
  101.9 0.8 finish.1
  (11 shorter events, 0.2 us)
Async XLA Ops:
  0.0 21.3 %collective-permute-start = (bf16[64,512]{1,0:T(8,128)(2,1)}, bf16[64,512]{1,0:T(8,128)(2,1)S(1)}, u32[]{:S(2)}, u32[]{:S(2)}) collective-permute-start(bf16[64,512]{1,0:T(8,128)(2,1)} %bitcast.18), channel_id=1, source_target_pairs={{0,64},{64,0},{1,65},{65,1},{2,66},{66,2},{3,67},{67,3},{4,68},{68... | collective-permute-start | bytes 196616 | tf_op jit(solution)/shard_map/ppermute | solution.py:170
  14.2 7.0 %copy-start.2 = (f32[512,16]{0,1:T(8,128)S(1)}, f32[512,16]{0,1:T(8,128)}, u32[]{:S(2)}) copy-start(f32[512,16]{0,1:T(8,128)} %param.9) | copy-start | bytes 98308
  14.2 15.1 %all-to-all-start = ((bf16[8,16,512]{2,1,0:T(8,128)(2,1)}), bf16[8,16,512]{2,1,0:T(8,128)(2,1)S(1)}, u32[]{:S(2)}, u32[]{:S(2)}) async-start(bf16[8,16,512]{2,1,0:T(8,128)(2,1)} %get-tuple-element.10), calls=%async_computation | async-start | bytes 262144 | tf_op jit(solution)/shard_map/all_to_all | solution.py:182
  21.2 0.8 copy-start.5
  22.1 12.3 %collective-permute-start.1 = (bf16[128,512]{1,0:T(8,128)(2,1)S(1)}, bf16[128,512]{1,0:T(8,128)(2,1)S(1)}, u32[]{:S(2)}, u32[]{:S(2)}) collective-permute-start(bf16[128,512]{1,0:T(8,128)(2,1)S(1)} %pad_maximum_fusion.2), channel_id=1, source_target_pairs={{0,32},{8,40},{16,48},{24,56},{32,0},{40,8},{48,16},{56,24},{1,33}... | collective-permute-start | bytes 393224 | tf_op jit(solution)/shard_map/ppermute | solution.py:170
  30.2 13.8 %copy-start.4 = (bf16[256,512]{1,0:T(8,128)(2,1)S(1)}, bf16[256,512]{1,0:T(8,128)(2,1)}, u32[]{:S(2)}) copy-start(bf16[256,512]{1,0:T(8,128)(2,1)} %gate_ref.1) | copy-start | bytes 786436
  30.2 13.6 %all-to-all-start.1 = ((bf16[8,16,512]{2,1,0:T(8,128)(2,1)}), bf16[8,16,512]{2,1,0:T(8,128)(2,1)S(1)}, u32[]{:S(2)}, u32[]{:S(2)}) async-start(bf16[8,16,512]{2,1,0:T(8,128)(2,1)} %broadcast_in_dim.32), calls=%async_computation.1 | async-start | bytes 262144 | tf_op jit(solution)/shard_map/all_to_all | solution.py:182
  34.4 9.6 %copy-start.1 = (bf16[256,512]{1,0:T(8,128)(2,1)S(1)}, bf16[256,512]{1,0:T(8,128)(2,1)}, u32[]{:S(2)}) copy-start(bf16[256,512]{1,0:T(8,128)(2,1)} %value_ref.3) | copy-start | bytes 786436
  34.4 9.6 %copy-start.3 = (f32[18,8,512]{2,1,0:T(8,128)S(1)}, f32[18,8,512]{2,1,0:T(8,128)}, u32[]{:S(2)}) copy-start(f32[18,8,512]{2,1,0:T(8,128)} %get-tuple-element.9.runs_ref) | copy-start | bytes 884740
  34.4 9.6 %copy-start = (bf16[256,512]{1,0:T(8,128)(2,1)S(1)}, bf16[256,512]{1,0:T(8,128)(2,1)}, u32[]{:S(2)}) copy-start(bf16[256,512]{1,0:T(8,128)(2,1)} %key_ref.3) | copy-start | bytes 786436
  34.5 24.2 %collective-permute-start.3 = (bf16[256,512]{1,0:T(8,128)(2,1)S(1)}, bf16[256,512]{1,0:T(8,128)(2,1)S(1)}, u32[]{:S(2)}, u32[]{:S(2)}) collective-permute-start(bf16[256,512]{1,0:T(8,128)(2,1)S(1)} %pad_maximum_fusion.1), channel_id=1, source_target_pairs={{56,0},{0,8},{8,16},{16,24},{24,32},{32,40},{40,48},{48,56},{57,1}... | collective-permute-start | bytes 786440 | tf_op jit(solution)/shard_map/ppermute | solution.py:174
  36.8 19.5 %collective-permute-start.2 = (bf16[256,512]{1,0:T(8,128)(2,1)S(1)}, bf16[256,512]{1,0:T(8,128)(2,1)S(1)}, u32[]{:S(2)}, u32[]{:S(2)}) collective-permute-start(bf16[256,512]{1,0:T(8,128)(2,1)S(1)} %pad_maximum_fusion.1), channel_id=1, source_target_pairs={{48,0},{56,8},{0,16},{8,24},{16,32},{24,40},{32,48},{40,56},{49,1}... | collective-permute-start | bytes 786440 | tf_op jit(solution)/shard_map/ppermute | solution.py:174
  47.0 22.4 %all-to-all-start.2 = ((bf16[8,128,512]{2,1,0:T(8,128)(2,1)}), bf16[8,128,512]{2,1,0:T(8,128)(2,1)S(1)}, u32[]{:S(2)}, u32[]{:S(2)}) async-start(bf16[8,128,512]{2,1,0:T(8,128)(2,1)} %bitcast.6), calls=%async_computation.2 | async-start | bytes 2097152 | tf_op jit(solution)/shard_map/all_to_all | solution.py:182
  54.3 9.7 %collective-permute-start.4 = (bf16[256,512]{1,0:T(8,128)(2,1)S(1)}, bf16[256,512]{1,0:T(8,128)(2,1)S(1)}, u32[]{:S(2)}, u32[]{:S(2)}) collective-permute-start(bf16[256,512]{1,0:T(8,128)(2,1)S(1)} %pad_maximum_fusion.1), channel_id=1, source_target_pairs={{8,0},{16,8},{24,16},{32,24},{40,32},{48,40},{56,48},{0,56},{9,1},... | collective-permute-start | bytes 786440 | tf_op jit(solution)/shard_map/ppermute | solution.py:174
  56.3 10.7 %collective-permute-start.5 = (bf16[512,512]{1,0:T(8,128)(2,1)S(1)}, bf16[512,512]{1,0:T(8,128)(2,1)S(1)}, u32[]{:S(2)}, u32[]{:S(2)}) collective-permute-start(bf16[512,512]{1,0:T(8,128)(2,1)S(1)} %pad_maximum_fusion.own_low), channel_id=1, source_target_pairs={{0,1},{1,0},{2,3},{3,2},{4,5},{5,4},{6,7},{7,6},{8,9},{9,8},{10,11... | collective-permute-start | bytes 1572872 | tf_op jit(solution)/shard_map/ppermute | solution.py:170
  64.1 4.3 %collective-permute-start.6 = (bf16[512,512]{1,0:T(8,128)(2,1)S(1)}, bf16[512,512]{1,0:T(8,128)(2,1)S(1)}, u32[]{:S(2)}, u32[]{:S(2)}) collective-permute-start(bf16[512,512]{1,0:T(8,128)(2,1)S(1)} %constant_dynamic-update-slice_fusion.own_high), channel_id=1, source_target_pairs={{0,1},{1,0},{2,3},{3,2},{4,5},{5,4},{6,7},{7,6},{8,9},{9,8},{10,11... | collective-permute-start | bytes 1572872 | tf_op jit(solution)/shard_map/ppermute | solution.py:170
